TPU v7x, 32 devices: a whole 2x2x4 slice. The times are simulated.
32 devices in a mesh: groups: 2 (over y), space: 8 (over z, x), dp: 2 (over core).
Axes of the slice: x: 2, y: 2, z: 4, core: 2. Of those that a mesh axis runs over, the one named last changes fastest.
Arguments:
- features: bfloat16 [4, 16, 8, 8, 512], P(('groups', 'dp'), 'space'), parts along dimension 0, may hold values from -6 to 6
- cotangent: bfloat16 [4, 16, 8, 8, 512], P(('groups', 'dp'), 'space'), parts along dimension 0, may hold values from -6 to 6
- kernel: bfloat16 [3, 3, 3, 64, 64], replicated, may hold values from -0.15625 to 0.15625
- neighbours: int32 [4, 16, 6], P(('groups', 'dp'), 'space'), parts along dimension 0, may hold values from -1 to 15, as said below
Outputs:
- response: bfloat16 [4, 16, 8, 8, 512], P(('groups', 'dp'), 'space'), parts along dimension 0
- feature_grad: bfloat16 [4, 16, 8, 8, 512], P(('groups', 'dp'), 'space'), parts along dimension 0
- kernel_grad: float32 [6, 3, 3, 64, 64], P('groups'), parts along dimension 0
There are 2 independent parts, one for each index of `groups`. A program takes and returns all parts, laid end to end along the dimension named above; an argument that names none is the same for every part. Nothing has to cross between parts.
Inputs may be any that keep to these rules, and one draw needn't show every extreme that they name: `neighbours`: the active bricks lie on a lattice of 3 by 8 by 4 bricks. Tile t sits at position p = t + 2: it covers lattice row p // 4 of the first dimension, rows 2 * (p % 4) to 2 * (p % 4) + 1 of the second and all rows of the third; it holds exactly 2 active bricks, in slots 2 * t to 2 * t + 1, listed by second then third lattice coordinate. In each realization one third-dimension row z is drawn, and every tile holds the bricks at z in its first and in its last second-dimension row; its other bricks are drawn at random. Directions are first dimension down, up, second down, up, third down, up; the relation is symmetric (if brick u is the up neighbour of s, s is the down neighbour of u), and -1 marks a neighbour that is inactive or outside the lattice.
All inputs are finite; a program needn't handle non-finite values.
Results may differ from a plain program's by a relative error of at most 0.0045.
Values may be sent and summed in bfloat16 or wider, within the bound.
A program may use at most 64 MiB of HBM per device.

v0:
```python
import math

import jax
import jax.numpy as jnp
from jax import lax
from jax.sharding import PartitionSpec as P

TILES_Y = 4


def shifted(x, axis, by):
    count = lax.axis_size(axis)
    pairs = [(i, i + by) for i in range(count) if 0 <= i + by < count]
    return lax.ppermute(x, axis, pairs)


def choose_rows(tables, shifts, column, source_device, flat_slot, present, position):
    stacked = jnp.concatenate(tables, axis=0)
    row_count = tables[0].shape[0]
    source_pick = jnp.zeros_like(flat_slot[:, column])
    for number, offset in enumerate(shifts):
        source_pick = jnp.where(source_device[:, column] == position + offset, number, source_pick)
    row_index = source_pick * row_count + flat_slot[:, column]
    picked = jnp.take(stacked, row_index, axis=0)
    present_rows = present[:, column].reshape((-1,) + (1,) * (picked.ndim - 1))
    return jnp.where(present_rows, picked, jnp.zeros_like(picked))


def make_banded(weights, channels):
    toeplitz = jnp.zeros((3, 3, 4, channels, 2, channels), jnp.bfloat16)
    for out_cell in range(2):
        for tap_z in range(3):
            toeplitz = toeplitz.at[:, :, out_cell + tap_z, :, out_cell, :].set(weights[:, :, tap_z])
    return toeplitz.reshape(3, 3, 4 * channels, 2 * channels)


def make_windows(extended, channels, pairs_z):
    return jnp.stack(
        [
            extended[..., 2 * channels * block_index : 2 * channels * block_index + 4 * channels]
            for block_index in range(pairs_z)
        ],
        axis=3,
    )


def correlate(windows, banded, rows_all, brick_edge, pairs_z, channels):
    result = jnp.zeros((rows_all, brick_edge, brick_edge, pairs_z, 2 * channels), jnp.float32)
    for row_offset in range(3):
        for col_offset in range(3):
            window_part = windows[
                :, row_offset : row_offset + brick_edge, col_offset : col_offset + brick_edge
            ]
            result = result + jnp.einsum(
                "nabjk,kc->nabjc",
                window_part,
                banded[row_offset, col_offset],
                preferred_element_type=jnp.float32,
            )
    return result


def body(features, cotangent, kernel, neighbours):
    realizations = features.shape[0]
    bricks = features.shape[1]
    brick_edge = features.shape[2]
    channels = kernel.shape[-1]
    rows_all = realizations * bricks
    tile_stride = TILES_Y
    pairs_z = brick_edge // 2
    position = lax.axis_index("space")
    neighbour_slots = neighbours.reshape(rows_all, 6)
    present = neighbour_slots >= 0
    safe_links = jnp.where(present, neighbour_slots, 0)
    source_device = safe_links // bricks
    base_rows = jnp.repeat(jnp.arange(realizations, dtype=jnp.int32) * bricks, bricks)[:, None]
    flat_slot = base_rows + safe_links % bricks

    def select(tables, shifts, column):
        return choose_rows(tables, shifts, column, source_device, flat_slot, present, position)

    volume = features.reshape(rows_all, brick_edge, brick_edge, brick_edge * channels)
    upper_face = volume[:, brick_edge - 1]
    lower_face = volume[:, 0]
    from_below = shifted(upper_face, "space", tile_stride)
    from_above = shifted(lower_face, "space", -tile_stride)
    below_part = select([upper_face, from_below], [0, -tile_stride], 0)
    above_part = select([lower_face, from_above], [0, tile_stride], 1)
    layered_x = jnp.concatenate([below_part[:, None], volume, above_part[:, None]], axis=1)
    upper_face = layered_x[:, :, brick_edge - 1]
    lower_face = layered_x[:, :, 0]
    from_below = shifted(upper_face, "space", 1)
    from_above = shifted(lower_face, "space", -1)
    below_part = select([upper_face, from_below], [0, -1], 2)
    above_part = select([lower_face, from_above], [0, 1], 3)
    layered_y = jnp.concatenate([below_part[:, :, None], layered_x, above_part[:, :, None]], axis=2)
    upper_face = layered_y[..., (brick_edge - 1) * channels :]
    lower_face = layered_y[..., :channels]
    extended = jnp.concatenate(
        [select([upper_face], [0], 4), layered_y, select([lower_face], [0], 5)], axis=-1
    )
    banded = make_banded(kernel, channels)
    windows = make_windows(extended, channels, pairs_z)
    result = correlate(windows, banded, rows_all, brick_edge, pairs_z, channels)
    response = result.reshape(features.shape).astype(jnp.bfloat16)
    cotangent_pairs = cotangent.reshape(rows_all, brick_edge, brick_edge, pairs_z, 2 * channels)
    band_terms = []
    for row_offset in range(3):
        for col_offset in range(3):
            window_part = windows[
                :, row_offset : row_offset + brick_edge, col_offset : col_offset + brick_edge
            ]
            band_terms.append(
                jnp.einsum(
                    "nabjk,nabjc->kc",
                    window_part,
                    cotangent_pairs,
                    preferred_element_type=jnp.float32,
                )
            )
    band_grad = jnp.stack(band_terms).reshape(3, 3, 4, channels, 2, channels)
    kernel_local = jnp.stack(
        [
            band_grad[:, :, tap_z, :, 0, :] + band_grad[:, :, tap_z + 1, :, 1, :]
            for tap_z in range(3)
        ],
        axis=2,
    )
    cells_all = rows_all * lax.axis_size("dp") * lax.axis_size("space") * brick_edge**3
    factor = 1.0 / math.sqrt(cells_all)
    kernel_grad = lax.psum(kernel_local, ("space", "dp")) * factor
    spread = jnp.zeros(
        (rows_all, brick_edge + 2, brick_edge + 2, pairs_z, 4 * channels), jnp.float32
    )
    for row_offset in range(3):
        for col_offset in range(3):
            contribution = jnp.einsum(
                "nabjc,kc->nabjk",
                cotangent_pairs,
                banded[row_offset, col_offset],
                preferred_element_type=jnp.float32,
            )
            spread = spread.at[
                :, row_offset : row_offset + brick_edge, col_offset : col_offset + brick_edge
            ].add(contribution)
    widened = jnp.zeros(
        (rows_all, brick_edge + 2, brick_edge + 2, (brick_edge + 2) * channels), jnp.float32
    )
    for block_index in range(pairs_z):
        widened = widened.at[
            ..., 2 * channels * block_index : 2 * channels * block_index + 4 * channels
        ].add(spread[..., block_index, :])
    lower_rim = widened[..., :channels]
    upper_rim = widened[..., (brick_edge + 1) * channels :]
    trimmed_z = widened[..., channels : (brick_edge + 1) * channels]
    trimmed_z = trimmed_z.at[..., (brick_edge - 1) * channels :].add(select([lower_rim], [0], 5))
    trimmed_z = trimmed_z.at[..., :channels].add(select([upper_rim], [0], 4))
    lower_rim = trimmed_z[:, :, 0]
    upper_rim = trimmed_z[:, :, brick_edge + 1]
    trimmed_y = trimmed_z[:, :, 1 : brick_edge + 1]
    from_below = shifted(upper_rim.astype(jnp.bfloat16), "space", 1).astype(upper_rim.dtype)
    from_above = shifted(lower_rim.astype(jnp.bfloat16), "space", -1).astype(lower_rim.dtype)
    trimmed_y = trimmed_y.at[:, :, brick_edge - 1].add(select([lower_rim, from_above], [0, 1], 3))
    trimmed_y = trimmed_y.at[:, :, 0].add(select([upper_rim, from_below], [0, -1], 2))
    lower_rim = trimmed_y[:, 0]
    upper_rim = trimmed_y[:, brick_edge + 1]
    trimmed_x = trimmed_y[:, 1 : brick_edge + 1]
    from_below = shifted(upper_rim.astype(jnp.bfloat16), "space", tile_stride).astype(
        upper_rim.dtype
    )
    from_above = shifted(lower_rim.astype(jnp.bfloat16), "space", -tile_stride).astype(
        lower_rim.dtype
    )
    trimmed_x = trimmed_x.at[:, brick_edge - 1].add(
        select([lower_rim, from_above], [0, tile_stride], 1)
    )
    trimmed_x = trimmed_x.at[:, 0].add(select([upper_rim, from_below], [0, -tile_stride], 0))
    feature_grad = trimmed_x.reshape(features.shape).astype(jnp.bfloat16)
    return (response, feature_grad, kernel_grad)


def solution(mesh):
    in_specs = (
        P(("groups", "dp"), "space", None, None, None),
        P(("groups", "dp"), "space", None, None, None),
        P(),
        P(("groups", "dp"), "space", None),
    )
    out_specs = (
        P(("groups", "dp"), "space", None, None, None),
        P(("groups", "dp"), "space", None, None, None),
        P("groups", None, None, None, None),
    )
    return jax.shard_map(body, mesh=mesh, in_specs=in_specs, out_specs=out_specs, check_vma=False)
```

profile of v0, /device:TPU:0, one launch (start us, length us, event | category | flops | bytes accessed | tf_op | source)
XLA Modules:
  0.0 196.4 jit_solution(7922815339144183871)
XLA Ops:
  7.2 0.8 slice_bitcast_fusion.10
  8.0 5.9 %collective-permute-start = (bf16[2,8,512]{2,1,0:T(8,128)(2,1)S(1)}, bf16[2,8,512]{2,1,0:T(8,128)(2,1)S(1)}, u32[]{:S(2)}, u32[]{:S(2)}) collective-permute-start(bf16[2,8,512]{2,1,0:T(8,128)(2,1)S(1)} %get-tuple-element.377), channel_id=1, source_target_pairs={{0,8},{2,10},{4,12},{6,14},{1,9},{3,11},{5,13},{7,15},{16,24},{18,... | collective-permute-start | bytes 49160 | tf_op jit(solution)/shard_map/ppermute | solution.py:14
  14.0 1.3 collective-permute-start.1
  15.3 0.7 bitcast_compare_fusion
  16.0 0.7 and_select_fusion.1
  16.7 0.3 slice_reduce_fusion.7
  17.0 0.6 fusion.134
  17.6 0.6 fusion.133
  18.1 0.9 slice_bitcast_fusion.6
  19.1 0.3 scatter.20
  19.5 1.2 copy.377
  20.7 0.5 reshape.1187
  21.4 0.7 and_reduce_fusion
  22.5 1.5 fusion.10
  24.0 2.8 %scatter-add.65 = f32[2,10,10,4,256]{4,2,1,0,3:T(8,128)S(1)} dynamic-update-slice(f32[2,10,10,4,256]{4,2,1,0,3:T(8,128)S(1)} %scatter-add.64, f32[2,8,8,4,256]{4,2,1,0,3:T(8,128)S(1)} %fusion.10, s32[]{:T(128)} %constant.794.clone.1, s32[]{:T(128)} %bitcast.54, s32[]{:T(128)} %bitcast.55, s32[]{:T(128)} %constant.794.clone.1, s32[]{:T(128)} %constant.794.clone.1) | dynamic-update-slice | bytes 1048580 | tf_op jit(solution)/shard_map/scatter-add | solution.py:145
  26.9 2.1 %fusion.9 = f32[2,8,8,4,256]{4,2,1,0,3:T(8,128)S(1)} fusion(f32[2,10,10,4,256]{4,2,1,0,3:T(8,128)S(1)} %scatter-add.65, s32[]{:T(128)} %bitcast.59, s32[]{:T(128)} %bitcast.60, pred[]{:T(512)} %and_reduce_fusion, bf16[3,3,256,128]{3,2,1,0:T(8,128)(2,1)S(1)} %reshape.1187, bf16[1,2,8,8,512]{4,3,2,1,0:T(8,128)(2,1)S(1)} %copy-done), kind=kOutput, calls=%fused_computation.28 | convolution fusion | flops 33816576 | bytes 1245193 | tf_op jit(solution)/shard_map/nabjc,kc->nabjk/dot_general | solution.py:137
  29.0 2.9 %scatter-add.66 = f32[2,10,10,4,256]{4,2,1,0,3:T(8,128)S(1)} dynamic-update-slice(f32[2,10,10,4,256]{4,2,1,0,3:T(8,128)S(1)} %scatter-add.65, f32[2,8,8,4,256]{4,2,1,0,3:T(8,128)S(1)} %fusion.9, s32[]{:T(128)} %constant.794.clone.1, s32[]{:T(128)} %bitcast.59, s32[]{:T(128)} %bitcast.60, s32[]{:T(128)} %constant.794.clone.1, s32[]{:T(128)} %constant.794.clone.1) | dynamic-update-slice | bytes 1048580 | tf_op jit(solution)/shard_map/scatter-add | solution.py:145
  31.9 0.3 fusion.7
  32.4 1.5 scatter-add.70
  34.2 1.5 scatter-add.71
  35.7 0.3 fusion.3
  36.3 1.5 scatter-add.75
  38.0 1.5 scatter-add.76
  40.2 0.3 slice_reduce_fusion.5
  40.5 0.6 gather_fusion.6
  41.2 0.6 gather_fusion.7
  41.7 3.1 %scatter-add.85 = f32[2,10,10,512]{3,2,1,0:T(8,128)S(1)} dynamic-update-slice(f32[2,10,10,512]{3,2,1,0:T(8,128)S(1)} %slice.1260, f32[2,10,10,64]{3,2,1,0:T(8,128)S(1)} %get-tuple-element.368, s32[]{:T(128)} %constant.794.clone.1, s32[]{:T(128)} %constant.794.clone.1, s32[]{:T(128)} %constant.794.clone.1, s32[]{:T(128)} %constant.811.clone.1) | dynamic-update-slice | bytes 102404 | tf_op jit(solution)/shard_map/scatter-add | solution.py:156
  45.0 0.5 scatter-add.86
  45.6 1.3 collective-permute-start.4
  46.9 4.5 %collective-permute-start.5 = (bf16[2,10,512]{2,0,1:T(2,128)(2,1)S(1)}, bf16[2,10,512]{2,0,1:T(2,128)(2,1)S(1)}, u32[]{:S(2)}, u32[]{:S(2)}) collective-permute-start(bf16[2,10,512]{2,0,1:T(2,128)(2,1)S(1)} %bitcast.421), channel_id=1, source_target_pairs={{0,2},{2,4},{4,6},{6,8},{8,10},{10,12},{12,14},{1,3},{3,5},{5,7},{... | collective-permute-start | bytes 61448 | tf_op jit(solution)/shard_map/ppermute | solution.py:14
  51.8 0.5 gather_fusion
  52.3 0.5 gather_fusion.1
  53.2 1.3 collective-permute-start.3
  54.5 4.9 %collective-permute-start.2 = (bf16[2,10,512]{2,1,0:T(8,128)(2,1)S(1)}, bf16[2,10,512]{2,1,0:T(8,128)(2,1)S(1)}, u32[]{:S(2)}, u32[]{:S(2)}) collective-permute-start(bf16[2,10,512]{2,1,0:T(8,128)(2,1)S(1)} %copy.364), channel_id=1, source_target_pairs={{0,2},{2,4},{4,6},{6,8},{8,10},{10,12},{12,14},{1,3},{3,5},{5,7},{... | collective-permute-start | bytes 61448 | tf_op jit(solution)/shard_map/ppermute | solution.py:14
  59.6 0.6 gather_fusion.8
  60.3 0.6 gather_fusion.9
  61.4 5.4 %collective-permute-start.7 = (bf16[2,8,512]{2,1,0:T(8,128)(2,1)S(1)}, bf16[2,8,512]{2,1,0:T(8,128)(2,1)S(1)}, u32[]{:S(2)}, u32[]{:S(2)}) collective-permute-start(bf16[2,8,512]{2,1,0:T(8,128)(2,1)S(1)} %get-tuple-element.365), channel_id=1, source_target_pairs={{0,8},{2,10},{4,12},{6,14},{1,9},{3,11},{5,13},{7,15},{16,24},{18,... | collective-permute-start | bytes 49160 | tf_op jit(solution)/shard_map/ppermute | solution.py:14
  66.9 1.5 collective-permute-start.6
  68.4 0.5 gather_fusion.3
  69.1 0.5 gather_fusion.2
  70.3 0.6 gather_fusion.4
  70.9 0.6 gather_fusion.5
  71.6 0.4 fusion.37
  72.3 1.4 fusion.129
  74.0 0.2 convolution_add_fusion.6
  74.7 0.2 convolution_add_fusion.3
  75.5 0.6 gather_fusion.11
  76.1 0.6 gather_fusion.10
  76.8 0.7 copy.421
  77.5 0.9 fusion.21
  78.4 0.9 fusion.20
  79.4 0.9 fusion.19
  80.3 0.9 fusion.18
  81.3 0.9 fusion.17
  82.2 0.9 fusion.16
  83.2 0.9 fusion.15
  84.1 0.9 fusion.14
  85.0 0.9 fusion.13
  85.9 2.7 %reshape.1202 = f32[3,3,4,64,2,64]{5,4,3,2,1,0:T(2,128)S(1)} reshape(f32[9,256,128]{2,1,0:T(8,128)} %fusion.13) | data formatting | bytes 2359296 | tf_op jit(solution)/shard_map/reshape | solution.py:121
  88.6 1.9 fusion.128
  90.7 1.0 pad_maximum_fusion
  91.7 1.7 fusion.12
  93.4 94.0 %all-reduce.5.cloned.1.call-done = f32[3,3,3,64,64]{4,3,2,1,0:T(8,128)} async-done(((f32[3,3,3,64,64]{4,3,2,1,0:T(8,128)}), f32[3,3,3,64,64]{4,3,2,1,0:T(8,128)}) %all-reduce.5.cloned.1.call-update) | async-done | bytes 442384 | tf_op jit(solution)/shard_map/psum | solution.py:131
  187.4 2.2 %broadcast_multiply_fusion = f32[3,3,3,64,64]{4,3,2,1,0:T(8,128)} fusion(f32[3,3,3,64,64]{4,3,2,1,0:T(8,128)} %all-reduce.5.cloned.1.call-done), kind=kLoop, calls=%fused_computation.62 | loop fusion | flops 110592 | bytes 884736 | tf_op jit(solution)/shard_map/mul | solution.py:131
  (130 shorter events, 6.6 us)
Async XLA Ops:
  7.2 14.9 %copy-start = (bf16[1,2,8,8,512]{4,3,2,1,0:T(8,128)(2,1)S(1)}, bf16[1,2,8,8,512]{4,3,2,1,0:T(8,128)(2,1)}, u32[]{:S(2)}) copy-start(bf16[1,2,8,8,512]{4,3,2,1,0:T(8,128)(2,1)} %param.67) | copy-start | bytes 393220
  7.2 12.2 %copy-start.2 = (bf16[3,3,3,64,64]{4,3,2,1,0:T(8,128)(2,1)S(1)}, bf16[3,3,3,64,64]{4,3,2,1,0:T(8,128)(2,1)}, u32[]{:S(2)}) copy-start(bf16[3,3,3,64,64]{4,3,2,1,0:T(8,128)(2,1)} %param.68) | copy-start | bytes 663556
  7.2 180.2 %all-reduce.5.cloned.1.call-start = ((), (), s32[]{:S(2)}) async-start(), calls=%async_computation | async-start | bytes 1769472 | tf_op jit(solution)/shard_map/psum | solution.py:131
  8.0 43.7 %collective-permute-start = (bf16[2,8,512]{2,1,0:T(8,128)(2,1)S(1)}, bf16[2,8,512]{2,1,0:T(8,128)(2,1)S(1)}, u32[]{:S(2)}, u32[]{:S(2)}) collective-permute-start(bf16[2,8,512]{2,1,0:T(8,128)(2,1)S(1)} %get-tuple-element.377), channel_id=1, source_target_pairs={{0,8},{2,10},{4,12},{6,14},{1,9},{3,11},{5,13},{7,15},{16,24},{18,... | collective-permute-start | bytes 49160 | tf_op jit(solution)/shard_map/ppermute | solution.py:14
  14.0 38.3 %collective-permute-start.1 = (bf16[2,8,512]{2,1,0:T(8,128)(2,1)S(1)}, bf16[2,8,512]{2,1,0:T(8,128)(2,1)S(1)}, u32[]{:S(2)}, u32[]{:S(2)}) collective-permute-start(bf16[2,8,512]{2,1,0:T(8,128)(2,1)S(1)} %get-tuple-element.378), channel_id=1, source_target_pairs={{8,0},{10,2},{12,4},{14,6},{9,1},{11,3},{13,5},{15,7},{24,16},{26,... | collective-permute-start | bytes 49160 | tf_op jit(solution)/shard_map/ppermute | solution.py:14
  20.7 0.7 copy-start.10
  21.4 53.8 %copy-start.1 = (bf16[3,3,256,128]{3,2,1,0:T(8,128)(2,1)}, bf16[3,3,256,128]{3,2,1,0:T(8,128)(2,1)S(1)}, u32[]{:S(2)}) copy-start(bf16[3,3,256,128]{3,2,1,0:T(8,128)(2,1)S(1)} %reshape.1187) | copy-start | bytes 1769476
  44.9 8.1 %copy-start.3 = (bf16[1,2,8,8,512]{4,3,2,1,0:T(8,128)(2,1)S(1)}, bf16[1,2,8,8,512]{4,3,2,1,0:T(8,128)(2,1)}, u32[]{:S(2)}) copy-start(bf16[1,2,8,8,512]{4,3,2,1,0:T(8,128)(2,1)} %param.66) | copy-start | bytes 393220
  45.6 13.9 %collective-permute-start.4 = (bf16[2,10,512]{2,0,1:T(2,128)(2,1)S(1)}, bf16[2,10,512]{2,0,1:T(2,128)(2,1)S(1)}, u32[]{:S(2)}, u32[]{:S(2)}) collective-permute-start(bf16[2,10,512]{2,0,1:T(2,128)(2,1)S(1)} %bitcast.420), channel_id=1, source_target_pairs={{2,0},{4,2},{6,4},{8,6},{10,8},{12,10},{14,12},{3,1},{5,3},{7,5},{... | collective-permute-start | bytes 61448 | tf_op jit(solution)/shard_map/ppermute | solution.py:14
  46.9 12.5 %collective-permute-start.5 = (bf16[2,10,512]{2,0,1:T(2,128)(2,1)S(1)}, bf16[2,10,512]{2,0,1:T(2,128)(2,1)S(1)}, u32[]{:S(2)}, u32[]{:S(2)}) collective-permute-start(bf16[2,10,512]{2,0,1:T(2,128)(2,1)S(1)} %bitcast.421), channel_id=1, source_target_pairs={{0,2},{2,4},{4,6},{6,8},{8,10},{10,12},{12,14},{1,3},{3,5},{5,7},{... | collective-permute-start | bytes 61448 | tf_op jit(solution)/shard_map/ppermute | solution.py:14
  53.2 15.2 %collective-permute-start.3 = (bf16[2,10,512]{2,1,0:T(8,128)(2,1)S(1)}, bf16[2,10,512]{2,1,0:T(8,128)(2,1)S(1)}, u32[]{:S(2)}, u32[]{:S(2)}) collective-permute-start(bf16[2,10,512]{2,1,0:T(8,128)(2,1)S(1)} %copy.368), channel_id=1, source_target_pairs={{2,0},{4,2},{6,4},{8,6},{10,8},{12,10},{14,12},{3,1},{5,3},{7,5},{... | collective-permute-start | bytes 61448 | tf_op jit(solution)/shard_map/ppermute | solution.py:14
  54.5 14.6 %collective-permute-start.2 = (bf16[2,10,512]{2,1,0:T(8,128)(2,1)S(1)}, bf16[2,10,512]{2,1,0:T(8,128)(2,1)S(1)}, u32[]{:S(2)}, u32[]{:S(2)}) collective-permute-start(bf16[2,10,512]{2,1,0:T(8,128)(2,1)S(1)} %copy.364), channel_id=1, source_target_pairs={{0,2},{2,4},{4,6},{6,8},{8,10},{10,12},{12,14},{1,3},{3,5},{5,7},{... | collective-permute-start | bytes 61448 | tf_op jit(solution)/shard_map/ppermute | solution.py:14
  61.4 14.0 %collective-permute-start.7 = (bf16[2,8,512]{2,1,0:T(8,128)(2,1)S(1)}, bf16[2,8,512]{2,1,0:T(8,128)(2,1)S(1)}, u32[]{:S(2)}, u32[]{:S(2)}) collective-permute-start(bf16[2,8,512]{2,1,0:T(8,128)(2,1)S(1)} %get-tuple-element.365), channel_id=1, source_target_pairs={{0,8},{2,10},{4,12},{6,14},{1,9},{3,11},{5,13},{7,15},{16,24},{18,... | collective-permute-start | bytes 49160 | tf_op jit(solution)/shard_map/ppermute | solution.py:14
  66.9 9.1 %collective-permute-start.6 = (bf16[2,8,512]{2,1,0:T(8,128)(2,1)S(1)}, bf16[2,8,512]{2,1,0:T(8,128)(2,1)S(1)}, u32[]{:S(2)}, u32[]{:S(2)}) collective-permute-start(bf16[2,8,512]{2,1,0:T(8,128)(2,1)S(1)} %get-tuple-element.366), channel_id=1, source_target_pairs={{8,0},{10,2},{12,4},{14,6},{9,1},{11,3},{13,5},{15,7},{24,16},{26,... | collective-permute-start | bytes 49160 | tf_op jit(solution)/shard_map/ppermute | solution.py:14
  75.4 2.1 %copy-start.9 = (bf16[2,8,8,4,256]{4,2,3,1,0:T(8,128)(2,1)S(1)}, bf16[2,8,8,4,256]{4,2,3,1,0:T(8,128)(2,1)}, u32[]{:S(2)}) copy-start(bf16[2,8,8,4,256]{4,2,3,1,0:T(8,128)(2,1)} %get-tuple-element.360) | copy-start | bytes 786436
  77.5 1.0 copy-start.8
  78.4 0.9 copy-start.7
  79.4 0.9 copy-start.6
  80.3 0.9 copy-start.5
  81.3 0.9 copy-start.4
Sparse Core Ops, SparseCore 0:
  91.8 95.5 all-reduce.4
where the time goes:
time: 197 us; the launch traced here: 196 us
  waiting for transfers between devices  94 us (48%)
  local copies, waits for them, and re-layouts  35.9 us (18%)
  starting transfers between devices  26.2 us (13%)
  matrix products  17.3 us (9%)
  between operations  15.1 us (8%)
  other arithmetic  7.91 us (4%)
    psum x1, waiting for transfers between devices, body(): kernel_grad = lax.psum(kernel_local, ('space', 'dp')) * factor  94 us
    ppermute x8, starting transfers between devices, shifted(): return lax.ppermute(x, axis, pairs)  26.2 us
    scatter-add x7, local copies, waits for them, and re-layouts, body(): spread = spread.at[:, row_offset:row_offset + brick_edge, col_offset:col_...  12 us
    dot_general x9, matrix products, body(): jnp.einsum('nabjk,nabjc->kc', window_part, cotangent_pairs, preferred_ele...  8.32 us
    gather x12, local copies, waits for them, and re-layouts, choose_rows(): picked = jnp.take(stacked, row_index, axis=0)  6.66 us
    dot_general x9, matrix products, body(): jnp.einsum('nabjc,kc->nabjk', cotangent_pairs, banded[row_offset, col_off...  5.35 us
  transfers between devices with their start and end apart: 9, of which 1 were waited for; matrix products, arithmetic and copies ran while one was open for 22% of the time, Pallas kernels for 0%

commit v1 on v0

v1 whole, which is shorter than its diff:
```python
import functools
import math

import jax
import jax.numpy as jnp
from jax import lax
from jax.experimental import pallas as pl
from jax.experimental.pallas import tpu as pltpu
from jax.sharding import PartitionSpec as P

TILES_Y = 4
EDGE = 8
CH = 64
PAIR = 2 * CH
PAIRS = EDGE // 2
ROWS = EDGE * CH
WIDE = ROWS + PAIR
TILES = 14
OWNED = TILES // 2
MESH = pl.DeviceIdType.MESH
DIAGONALS = [(side, dx) for side in range(2) for dx in range(3)]


def low_lanes(shape):
    return lax.broadcasted_iota(jnp.int32, shape, len(shape) - 1) < CH


def in_range(tile, count):
    return (tile >= 0) & (tile < count)


def receives(tile, dx, dy, count, first_x):
    column = (tile + TILES_Y // 2) % TILES_Y + dy
    there = in_range(tile + TILES_Y * dx + dy, count) & (column >= 0) & (column < TILES_Y)
    between = tile + TILES_Y * dx if first_x else tile + dy
    return in_range(tile, count) & in_range(between, count) & there


def place_windows(store, center, edge):
    low = low_lanes((center.shape[0], PAIR))
    pairs = [center[:, PAIR * k : PAIR * (k + 1)] for k in range(PAIRS)]
    for k in range(PAIRS):
        after = pairs[k + 1] if k + 1 < PAIRS else edge
        before = pairs[k - 1] if k > 0 else edge
        store(k, jnp.where(low, after, before), pairs[k])


def build_windows(out_ref, center, edge, halo_low, halo_high, edge_low, edge_high):
    planes = center.shape[0]

    def flat(values):
        return values.reshape(planes * EDGE, values.shape[-1])

    def shifted(values, low_row, high_row, tap):
        if tap == 0:
            return jnp.concatenate([low_row, values[:, : EDGE - 1]], axis=1)
        if tap == 2:
            return jnp.concatenate([values[:, 1:], high_row], axis=1)
        return values

    for tap in range(3):
        moved = flat(shifted(center, halo_low, halo_high, tap))
        moved_edge = flat(shifted(edge, edge_low, edge_high, tap))

        def store(k, around, pair):
            rows = pl.ds(k * planes * EDGE, planes * EDGE)
            base = tap * 2 * PAIR
            out_ref[rows, base : base + PAIR] = around.astype(jnp.bfloat16)
            out_ref[rows, base + PAIR : base + 2 * PAIR] = pair.astype(jnp.bfloat16)

        place_windows(store, moved, moved_edge)


def outer_rows(center, y_ref, width):
    low, high = [], []
    for side in range(2):
        below = y_ref[side, 0].astype(jnp.float32)[EDGE - 1 :, None, :width]
        level = y_ref[side, 1].astype(jnp.float32)[:, None, :width]
        above = y_ref[side, 2].astype(jnp.float32)[:1, None, :width]
        (low if side == 0 else high).extend([below, level, above])
    planes = EDGE + 2
    low.append(center[:planes, EDGE - 1 :])
    high = [center[planes:, :1]] + high
    return jnp.concatenate(low, axis=0), jnp.concatenate(high, axis=0)


def sum_taps(result, planes, store):
    for k in range(PAIRS):
        for brick in range(2):
            base = k * planes * EDGE + brick * (planes // 2) * EDGE
            total = result[base : base + EDGE * EDGE, :PAIR]
            for a in range(1, 3):
                start = base + a * EDGE
                total = total + result[start : start + EDGE * EDGE, a * PAIR : (a + 1) * PAIR]
            store(brick, k, total.reshape(EDGE, EDGE, PAIR).astype(jnp.bfloat16))


def kernel_body(
    count, dp_count, scale, reduce_here,
    nb_ref, f_ref, c_ref, w_ref,
    resp_ref, fg_ref, kg_ref,
    fx, fy, cx, cy, fys, cys, cz, xw, cw, wf, wg, part, core_in, sbuf, rbuf, fin,
    halo_send, halo_recv, core_sem, rs_send, rs_recv, ag_send, ag_recv, fw_send, fw_recv,
):
    me = lax.axis_index("space")
    core = lax.axis_index("dp")
    planes = 2 * (EDGE + 2)

    fx[...] = jnp.zeros_like(fx)
    fy[...] = jnp.zeros_like(fy)
    cx[...] = jnp.zeros_like(cx)
    cy[...] = jnp.zeros_like(cy)

    barrier = pltpu.get_barrier_semaphore()
    if reduce_here:
        for step in range(1, count):
            pl.semaphore_signal(
                barrier, inc=1, device_id={"space": (me + step) % count}, device_id_type=MESH
            )
        pl.semaphore_signal(barrier, inc=1, device_id={"dp": 1 - core}, device_id_type=MESH)
    else:
        for step in (1, 3, 4, 5):
            for other in (me + step, me - step):

                @pl.when(in_range(other, count))
                def _():
                    pl.semaphore_signal(
                        barrier, inc=1, device_id={"space": other}, device_id_type=MESH
                    )

    for brick in range(2):
        other = 1 - brick
        before = jnp.where(nb_ref[0, brick, 4] >= 0, 1.0, 0.0)
        after = jnp.where(nb_ref[0, brick, 5] >= 0, 1.0, 0.0)
        cz[brick, :, :, :ROWS] = c_ref[0, brick]
        low = low_lanes((EDGE, EDGE, PAIR))
        edge = jnp.where(
            low,
            c_ref[0, other, :, :, :PAIR].astype(jnp.float32) * after,
            c_ref[0, other, :, :, ROWS - PAIR :].astype(jnp.float32) * before,
        )
        cz[brick, :, :, ROWS:] = edge.astype(jnp.bfloat16)
    fys[0] = f_ref[0, 1].astype(jnp.float32)[:, EDGE - 1].astype(jnp.bfloat16)
    fys[1] = f_ref[0, 0].astype(jnp.float32)[:, 0].astype(jnp.bfloat16)
    cys[0] = cz[1].astype(jnp.float32)[:, EDGE - 1].astype(jnp.bfloat16)
    cys[1] = cz[0].astype(jnp.float32)[:, 0].astype(jnp.bfloat16)

    if reduce_here:
        pl.semaphore_wait(barrier, count)
    else:
        for step in (1, 3, 4, 5):
            for other in (me + step, me - step):

                @pl.when(in_range(other, count))
                def _():
                    pl.semaphore_wait(barrier, 1)

    def halo(kind):
        x_ref, y_ref, ys_ref = ((fx, fy, fys), (cx, cy, cys))[kind]
        entries = []
        for side in range(2):
            dx = 2 * side - 1
            target = me - TILES_Y * dx
            face = EDGE - 1 if side == 0 else 0
            source = f_ref.at[0, :, face] if kind == 0 else cz.at[:, face]
            entries.append((
                receives(target, dx, 0, count, True),
                receives(me, dx, 0, count, True),
                source, x_ref.at[side], target,
            ))
        for side, column in DIAGONALS:
            dx, dy = column - 1, 2 * side - 1
            target = me - TILES_Y * dx - dy
            entries.append((
                receives(target, dx, dy, count, kind == 1),
                receives(me, dx, dy, count, kind == 1),
                ys_ref.at[side], y_ref.at[side, column], target,
            ))
        out = []
        for number, (sent, arrives, source, target_ref, target) in enumerate(entries):
            out.append((sent, arrives, pltpu.make_async_remote_copy(
                src_ref=source, dst_ref=target_ref,
                send_sem=halo_send.at[kind * 8 + number],
                recv_sem=halo_recv.at[kind * 8 + number],
                device_id={"space": target}, device_id_type=MESH,
            )))
        return out

    def start_halo(copies):
        for sent, _, copy in copies:
            pl.when(sent)(copy.start)

    def wait_halo(copies):
        for _, arrives, copy in copies:
            pl.when(arrives)(copy.wait_recv)

    f_copies, c_copies = halo(0), halo(1)
    start_halo(f_copies)
    start_halo(c_copies)

    order = (3, 0, 1, 2)
    blank = jnp.zeros((CH, CH), jnp.bfloat16)
    for a in range(3):
        for b in range(3):
            taps = [w_ref[a, b, d] for d in range(3)]
            for slot, w in enumerate(order):
                left = taps[w] if w < 3 else blank
                right = taps[w - 1] if w > 0 else blank
                row = b * 4 * CH + slot * CH
                wf[row : row + CH, a * PAIR : (a + 1) * PAIR] = jnp.concatenate([left, right], axis=1)
            flip_a, flip_b = 2 - a, 2 - b
            for cell in range(2):
                row = flip_a * PAIR + cell * CH
                for half in range(2):
                    pieces = []
                    for w in order[2 * half : 2 * half + 2]:
                        d = w - cell
                        pieces.append(taps[2 - d] if 0 <= d <= 2 else blank)
                    lane = flip_b * 4 * CH + half * PAIR
                    wg[row : row + CH, lane : lane + PAIR] = jnp.concatenate(pieces, axis=1)

    wait_halo(f_copies)

    def stack(values, x_ref, width):
        parts = []
        for brick in range(2):
            parts.append(x_ref[0, brick].astype(jnp.float32)[None, :, :width])
            parts.append(values[brick])
            parts.append(x_ref[1, brick].astype(jnp.float32)[None, :, :width])
        return jnp.concatenate(parts, axis=0)

    center = stack([f_ref[0, b].astype(jnp.float32) for b in range(2)], fx, ROWS)
    row_low, row_high = outer_rows(center, fy, ROWS)

    def third_edge(values):
        pieces = []
        half = planes // 2
        for brick in range(2):
            other = values[(1 - brick) * half : (2 - brick) * half]
            before = jnp.where(nb_ref[0, brick, 4] >= 0, 1.0, 0.0)
            after = jnp.where(nb_ref[0, brick, 5] >= 0, 1.0, 0.0)
            low = low_lanes((half, values.shape[1], PAIR))
            pieces.append(
                jnp.where(low, other[..., :PAIR] * after, other[..., ROWS - PAIR :] * before)
            )
        return jnp.concatenate(pieces, axis=0)

    build_windows(
        xw, center, third_edge(center), row_low, row_high, third_edge(row_low), third_edge(row_high)
    )

    cot_rows = []
    zero_plane = jnp.zeros((EDGE, PAIR), jnp.float32)
    for k in range(PAIRS):
        per_tap = []
        blocks = [
            c_ref[0, brick, :, :, k * PAIR : (k + 1) * PAIR].astype(jnp.float32).reshape(EDGE * EDGE, PAIR)
            for brick in range(2)
        ]
        for a in range(3):
            pieces = []
            for brick in range(2):
                pieces += [zero_plane] * a + [blocks[brick]] + [zero_plane] * (2 - a)
            per_tap.append(jnp.concatenate(pieces, axis=0))
        cot_rows.append(jnp.concatenate(per_tap, axis=1).astype(jnp.bfloat16))
    cot_all = jnp.concatenate(cot_rows, axis=0)
    grad = lax.dot_general(
        cot_all, xw[...], (((0,), (0,)), ((), ())), preferred_element_type=jnp.float32
    )
    low = low_lanes((CH, PAIR))
    first_taps = []
    for a in range(3):
        for b in range(3):
            cell0 = grad[a * PAIR : a * PAIR + CH, b * 4 * CH : (b + 1) * 4 * CH]
            cell1 = grad[a * PAIR + CH : (a + 1) * PAIR, b * 4 * CH : (b + 1) * 4 * CH]
            turned0 = pltpu.roll(cell1[:, :PAIR], CH, 1)
            turned1 = pltpu.roll(cell1[:, PAIR:], CH, 1)
            part[a * 3 + b] = cell0[:, PAIR:] + jnp.where(low, turned1, turned0)
            first_taps.append(cell0[:, :PAIR] + turned1)
    for m in range(5):
        high = first_taps[2 * m + 1] if 2 * m + 1 < 9 else jnp.zeros((CH, PAIR), jnp.float32)
        part[9 + m] = jnp.where(low, pltpu.roll(first_taps[2 * m], CH, 1), high)

    if reduce_here:
        core_copy = pltpu.make_async_remote_copy(
            src_ref=part.at[pl.ds((1 - core) * OWNED, OWNED)], dst_ref=core_in,
            send_sem=core_sem.at[0], recv_sem=core_sem.at[1],
            device_id={"dp": 1 - core}, device_id_type=MESH,
        )
        core_copy.start()

    result = jnp.dot(xw[...], wf[...], preferred_element_type=jnp.float32)

    def put_response(brick, k, value):
        resp_ref[0, brick, :, :, k * PAIR : (k + 1) * PAIR] = value

    sum_taps(result, planes, put_response)

    if reduce_here:
        core_copy.wait()
        rs_copies = []
        for tile in range(OWNED):
            sbuf[tile] = (part[core * OWNED + tile] + core_in[tile]).astype(jnp.bfloat16)
            copy = pltpu.make_async_remote_copy(
                src_ref=sbuf.at[tile], dst_ref=rbuf.at[me],
                send_sem=rs_send.at[tile], recv_sem=rs_recv.at[me],
                device_id={"space": tile}, device_id_type=MESH,
            )
            rs_copies.append(copy)

            @pl.when(me != tile)
            def _():
                copy.start()

            @pl.when(me == tile)
            def _():
                rbuf[tile] = sbuf[tile]

    wait_halo(c_copies)
    wide = stack([cz[b].astype(jnp.float32) for b in range(2)], cx, WIDE)
    wide_low, wide_high = outer_rows(wide, cy, WIDE)
    build_windows(
        cw, wide[..., :ROWS], wide[..., ROWS:], wide_low[..., :ROWS], wide_high[..., :ROWS],
        wide_low[..., ROWS:], wide_high[..., ROWS:],
    )
    result = lax.dot_general(
        cw[...], wg[...], (((1,), (1,)), ((), ())), preferred_element_type=jnp.float32
    )

    def put_gradient(brick, k, value):
        fg_ref[0, brick, :, :, k * PAIR : (k + 1) * PAIR] = value

    sum_taps(result, planes, put_gradient)

    def finish(tile, value):
        turned = (value * scale).T
        if tile < 9:
            kg_ref[tile // 3, tile % 3, 1] = turned[:CH]
            kg_ref[tile // 3, tile % 3, 2] = turned[CH:]
        else:
            for half in range(2):
                tap = 2 * (tile - 9) + half
                if tap < 9:
                    kg_ref[tap // 3, tap % 3, 0] = turned[half * CH : (half + 1) * CH]

    if reduce_here:
        for tile in range(OWNED):
            pl.when(me != tile)(rs_copies[tile].wait_send)

        def gather_copy(step):
            target = (me + step) % count
            return pltpu.make_async_remote_copy(
                src_ref=fin.at[core * OWNED + me], dst_ref=fin.at[core * OWNED + me],
                send_sem=ag_send.at[step], recv_sem=ag_recv.at[me],
                device_id={"space": target}, device_id_type=MESH,
            )

        def forward_copy(tile):
            spot = fin.at[core * OWNED + tile]
            return pltpu.make_async_remote_copy(
                src_ref=spot, dst_ref=spot,
                send_sem=fw_send.at[tile], recv_sem=fw_recv.at[tile],
                device_id={"dp": 1 - core}, device_id_type=MESH,
            )

        @pl.when(me < OWNED)
        def _():
            total = jnp.zeros((CH, PAIR), jnp.float32)
            for source in range(count):

                @pl.when(me != source)
                def _():
                    pltpu.make_async_remote_copy(
                        src_ref=sbuf.at[0], dst_ref=rbuf.at[source],
                        send_sem=rs_send.at[0], recv_sem=rs_recv.at[source],
                        device_id={"space": source}, device_id_type=MESH,
                    ).wait_recv()

                total = total + rbuf[source].astype(jnp.float32)
            fin[core * OWNED + me] = total.astype(jnp.bfloat16)
            for step in range(1, count):
                gather_copy(step).start()

        for tile in range(OWNED):

            @pl.when(me != tile)
            def _():
                spot = fin.at[core * OWNED + tile]
                pltpu.make_async_remote_copy(
                    src_ref=spot, dst_ref=spot,
                    send_sem=ag_send.at[0], recv_sem=ag_recv.at[tile],
                    device_id={"space": tile}, device_id_type=MESH,
                ).wait_recv()

            forward_copy(tile).start()

        for tile in range(OWNED):
            spot = fin.at[(1 - core) * OWNED + tile]
            pltpu.make_async_remote_copy(
                src_ref=spot, dst_ref=spot,
                send_sem=fw_send.at[tile], recv_sem=fw_recv.at[tile],
                device_id={"dp": 1 - core}, device_id_type=MESH,
            ).wait_recv()
        for tile in range(TILES):
            finish(tile, fin[tile].astype(jnp.float32))
        for tile in range(OWNED):
            forward_copy(tile).wait_send()

        @pl.when(me < OWNED)
        def _():
            for step in range(1, count):
                gather_copy(step).wait_send()
    else:
        for tile in range(TILES):
            finish(tile, part[tile])
    for sent, _, copy in f_copies + c_copies:
        pl.when(sent)(copy.wait_send)


def body(features, cotangent, kernel, neighbours):
    count = lax.axis_size("space")
    dp_count = lax.axis_size("dp")
    reduce_here = count == 8 and dp_count == 2
    cells = features.shape[0] * features.shape[1] * dp_count * count * EDGE**3
    scale = 1.0 / math.sqrt(cells)
    bf16, f32 = jnp.bfloat16, jnp.float32
    planes = 2 * (EDGE + 2)
    rows = PAIRS * planes * EDGE
    dma = pltpu.SemaphoreType.DMA
    vmem = pl.BlockSpec(memory_space=pltpu.VMEM)
    response, feature_grad, kernel_grad = pl.pallas_call(
        functools.partial(kernel_body, count, dp_count, scale, reduce_here),
        out_shape=(
            jax.ShapeDtypeStruct(features.shape, bf16),
            jax.ShapeDtypeStruct(features.shape, bf16),
            jax.ShapeDtypeStruct(kernel.shape, f32),
        ),
        in_specs=[pl.BlockSpec(memory_space=pltpu.SMEM), vmem, vmem, vmem],
        out_specs=(vmem, vmem, vmem),
        scratch_shapes=[
            pltpu.VMEM((2, 2, EDGE, ROWS), bf16),
            pltpu.VMEM((2, 3, EDGE, ROWS), bf16),
            pltpu.VMEM((2, 2, EDGE, WIDE), bf16),
            pltpu.VMEM((2, 3, EDGE, WIDE), bf16),
            pltpu.VMEM((2, EDGE, ROWS), bf16),
            pltpu.VMEM((2, EDGE, WIDE), bf16),
            pltpu.VMEM((2, EDGE, EDGE, WIDE), bf16),
            pltpu.VMEM((rows, 12 * CH), bf16),
            pltpu.VMEM((rows, 12 * CH), bf16),
            pltpu.VMEM((12 * CH, 6 * CH), bf16),
            pltpu.VMEM((6 * CH, 12 * CH), bf16),
            pltpu.VMEM((TILES, CH, PAIR), f32),
            pltpu.VMEM((OWNED, CH, PAIR), f32),
            pltpu.VMEM((OWNED, CH, PAIR), bf16),
            pltpu.VMEM((8, CH, PAIR), bf16),
            pltpu.VMEM((TILES, CH, PAIR), bf16),
            dma((16,)), dma((16,)), dma((2,)), dma((8,)), dma((8,)),
            dma((8,)), dma((8,)), dma((8,)), dma((8,)),
        ],
        compiler_params=pltpu.CompilerParams(
            collective_id=0, has_side_effects=True, vmem_limit_bytes=40 * 1024 * 1024
        ),
        cost_estimate=pl.CostEstimate(flops=10**9, bytes_accessed=2 * 10**6, transcendentals=0),
    )(neighbours, features, cotangent, kernel)
    if not reduce_here:
        kernel_grad = lax.psum(kernel_grad, ("space", "dp"))
    return (response, feature_grad, kernel_grad)


def solution(mesh):
    in_specs = (
        P(("groups", "dp"), "space", None, None, None),
        P(("groups", "dp"), "space", None, None, None),
        P(),
        P(("groups", "dp"), "space", None),
    )
    out_specs = (
        P(("groups", "dp"), "space", None, None, None),
        P(("groups", "dp"), "space", None, None, None),
        P("groups", None, None, None, None),
    )
    return jax.shard_map(body, mesh=mesh, in_specs=in_specs, out_specs=out_specs, check_vma=False)
```

time: 197 us -> 29.9 us (0.15)
  waiting for transfers between devices: 94 us -> 0 us
  local copies, waits for them, and re-layouts: 35.9 us -> 5.72 us
  starting transfers between devices: 26.2 us -> 0 us
  Pallas kernels: 0 us -> 23.1 us
  matrix products: 17.3 us -> 0 us
  between operations: 15.1 us -> 0.65 us
  other arithmetic: 7.91 us -> 0 us
    psum x1 -> x0, waiting for transfers between devices: 94 us -> none  [body(): kernel_grad = lax.psum(kernel_local, ('space', 'dp')) * factor]
    ppermute x8 -> x0, starting transfers between devices: 26.2 us -> none  [shifted(): return lax.ppermute(x, axis, pairs)]
    pallas_call x0 -> x1, Pallas kernels: none -> 23.1 us  [body(): pl.pallas_call(functools.partial(kernel_body, count, dp_count, scale, red...]
    dot_general x27 -> x0, matrix products: 17.3 us -> none  [the longest x9 8.32 us: body(): jnp.einsum('nabjk,nabjc->kc', window_part, cotangent_pairs, preferred_ele...]
    scatter-add x13 -> x0, local copies, waits for them, and re-layouts: 16 us -> none  [the longest x7 12 us: body(): spread = spread.at[:, row_offset:row_offset + brick_edge, col_offset:col_...]
    gather x12 -> x0, local copies, waits for them, and re-layouts: 6.66 us -> none  [choose_rows(): picked = jnp.take(stacked, row_index, axis=0)]
    unnamed x25 -> x11, local copies, waits for them, and re-layouts: 0.95 us -> 5.72 us
    slice x15 -> x0, local copies, waits for them, and re-layouts: 4.17 us -> none  [the longest x1 1.91 us: body(): band_grad[:, :, tap_z + 1, :, 1, :]]
  transfers between devices with their start and end apart: 9 -> 0, of which waited for: 1 -> 0; matrix products, arithmetic and copies ran while one was open for 22% -> 0% of each run, Pallas kernels for 0% -> 0%
where the time goes in v1:
time: 29.9 us; the launch traced here: 29.5 us
  Pallas kernels  23.1 us (77%)
  local copies, waits for them, and re-layouts  5.72 us (19%)
  between operations  0.65 us (2%)
    pallas_call x1, Pallas kernels, body(): pl.pallas_call(functools.partial(kernel_body, count, dp_count, scale, red...  23.1 us
    unnamed x11, local copies, waits for them, and re-layouts  5.72 us

profile of v1, /device:TPU:0, one launch (start us, length us, event | category | flops | bytes accessed | tf_op | source)
XLA Modules:
  0.0 29.5 jit_solution(11488377653454802527)
XLA Ops:
  0.6 0.0 copy-start
  0.6 1.0 %copy-done = bf16[3,3,3,64,64]{4,3,2,1,0:T(8,128)(2,1)S(1)} copy-done((bf16[3,3,3,64,64]{4,3,2,1,0:T(8,128)(2,1)S(1)}, bf16[3,3,3,64,64]{4,3,2,1,0:T(8,128)(2,1)}, u32[]{:S(2)}) %copy-start) | copy-done | bytes 221208
  1.6 0.0 copy-start.1
  1.6 0.9 %copy-done.1 = bf16[1,2,8,8,512]{4,3,2,1,0:T(8,128)(2,1)S(1)} copy-done((bf16[1,2,8,8,512]{4,3,2,1,0:T(8,128)(2,1)S(1)}, bf16[1,2,8,8,512]{4,3,2,1,0:T(8,128)(2,1)}, u32[]{:S(2)}) %copy-start.1) | copy-done | bytes 131096
  2.5 0.0 copy-start.2
  2.6 0.9 %copy-done.2 = bf16[1,2,8,8,512]{4,3,2,1,0:T(8,128)(2,1)S(1)} copy-done((bf16[1,2,8,8,512]{4,3,2,1,0:T(8,128)(2,1)S(1)}, bf16[1,2,8,8,512]{4,3,2,1,0:T(8,128)(2,1)}, u32[]{:S(2)}) %copy-start.2) | copy-done | bytes 131096
  3.5 0.0 copy-start.3
  3.5 0.7 %copy-done.3 = s32[1,2,6]{2,1,0:T(2,128)S(1)} copy-done((s32[1,2,6]{2,1,0:T(2,128)S(1)}, s32[1,2,6]{2,1,0:T(2,128)}, u32[]{:S(2)}) %copy-start.3) | copy-done | bytes 72
  4.1 23.1 %shard_map.67 = (bf16[1,2,8,8,512]{4,3,2,1,0:T(8,128)(2,1)S(1)}, bf16[1,2,8,8,512]{4,3,2,1,0:T(8,128)(2,1)S(1)}, f32[3,3,3,64,64]{4,3,2,1,0:T(8,128)S(1)}) custom-call(s32[1,2,6]{2,1,0:T(2,128)S(1)} %copy-done.3, bf16[1,2,8,8,512]{4,3,2,1,0:T(8,128)(2,1)S(1)} %copy-done.1, bf16[1,2,8,8,512]{4,3,2,1,0:T(8,128)(2,1)S(1)} %copy-done.2, ...), custom_call_target="tpu_custom_call" | custom-call | flops 1000000000 | bytes 2000000 | tf_op jit(solution)/shard_map/pallas_call | solution.py:431
  27.3 0.7 %copy.10 = bf16[1,2,8,8,512]{4,3,2,1,0:T(8,128)(2,1)} copy(bf16[1,2,8,8,512]{4,3,2,1,0:T(8,128)(2,1)S(1)} %get-tuple-element.6) | data formatting | bytes 262144
  27.9 0.7 %copy.11 = bf16[1,2,8,8,512]{4,3,2,1,0:T(8,128)(2,1)} copy(bf16[1,2,8,8,512]{4,3,2,1,0:T(8,128)(2,1)S(1)} %get-tuple-element.7) | data formatting | bytes 262144
  28.6 0.9 %copy.12 = f32[3,3,3,64,64]{4,3,2,1,0:T(8,128)} copy(f32[3,3,3,64,64]{4,3,2,1,0:T(8,128)S(1)} %get-tuple-element.8) | data formatting | bytes 884736
Async XLA Ops:
  0.6 1.0 %copy-start = (bf16[3,3,3,64,64]{4,3,2,1,0:T(8,128)(2,1)S(1)}, bf16[3,3,3,64,64]{4,3,2,1,0:T(8,128)(2,1)}, u32[]{:S(2)}) copy-start(bf16[3,3,3,64,64]{4,3,2,1,0:T(8,128)(2,1)} %w_ref.1) | copy-start | bytes 663556
  1.6 0.9 %copy-start.1 = (bf16[1,2,8,8,512]{4,3,2,1,0:T(8,128)(2,1)S(1)}, bf16[1,2,8,8,512]{4,3,2,1,0:T(8,128)(2,1)}, u32[]{:S(2)}) copy-start(bf16[1,2,8,8,512]{4,3,2,1,0:T(8,128)(2,1)} %f_ref.1) | copy-start | bytes 393220
  2.5 0.9 %copy-start.2 = (bf16[1,2,8,8,512]{4,3,2,1,0:T(8,128)(2,1)S(1)}, bf16[1,2,8,8,512]{4,3,2,1,0:T(8,128)(2,1)}, u32[]{:S(2)}) copy-start(bf16[1,2,8,8,512]{4,3,2,1,0:T(8,128)(2,1)} %c_ref.1) | copy-start | bytes 393220
  3.5 0.7 %copy-start.3 = (s32[1,2,6]{2,1,0:T(2,128)S(1)}, s32[1,2,6]{2,1,0:T(2,128)}, u32[]{:S(2)}) copy-start(s32[1,2,6]{2,1,0:T(2,128)} %nb_ref.1) | copy-start | bytes 148

commit v2 on v1

--- a/solution.py
+++ b/solution.py
@@ -45,7 +45,7 @@
         store(k, jnp.where(low, after, before), pairs[k])
 
 
-def build_windows(out_ref, center, edge, halo_low, halo_high, edge_low, edge_high):
+def window_builder(out_ref, center, edge, halo_low, halo_high, edge_low, edge_high):
     planes = center.shape[0]
 
     def flat(values):
@@ -58,7 +58,7 @@
             return jnp.concatenate([values[:, 1:], high_row], axis=1)
         return values
 
-    for tap in range(3):
+    def build(tap):
         moved = flat(shifted(center, halo_low, halo_high, tap))
         moved_edge = flat(shifted(edge, edge_low, edge_high, tap))
 
@@ -69,6 +69,8 @@
             out_ref[rows, base + PAIR : base + 2 * PAIR] = pair.astype(jnp.bfloat16)
 
         place_windows(store, moved, moved_edge)
+
+    return build
 
 
 def outer_rows(center, y_ref, width):
@@ -96,15 +98,29 @@
 
 
 def kernel_body(
-    count, dp_count, scale, reduce_here,
+    count, reduce_here,
+    nb_hbm, f_hbm, c_hbm, w_hbm,
+    resp_ref, fg_ref, tiles_ref,
     nb_ref, f_ref, c_ref, w_ref,
-    resp_ref, fg_ref, kg_ref,
-    fx, fy, cx, cy, fys, cys, cz, xw, cw, wf, wg, part, core_in, sbuf, rbuf, fin,
-    halo_send, halo_recv, core_sem, rs_send, rs_recv, ag_send, ag_recv, fw_send, fw_recv,
+    fx, fy, cx, cy, fys, cys, cz, xw, cw, ct, wf, wg, part, core_in, sbuf, rbuf,
+    load_sem, halo_send, halo_recv, core_sem, rs_send, rs_recv, ag_send, ag_recv, fw_send, fw_recv,
 ):
     me = lax.axis_index("space")
     core = lax.axis_index("dp")
     planes = 2 * (EDGE + 2)
+
+    if reduce_here:
+        fin = tiles_ref
+    else:
+        part = tiles_ref
+    loads = [
+        pltpu.make_async_copy(src, dst, load_sem.at[number])
+        for number, (src, dst) in enumerate(
+            [(f_hbm, f_ref), (c_hbm, c_ref), (nb_hbm, nb_ref), (w_hbm, w_ref)]
+        )
+    ]
+    for load in loads:
+        load.start()
 
     fx[...] = jnp.zeros_like(fx)
     fy[...] = jnp.zeros_like(fy)
@@ -127,33 +143,6 @@
                     pl.semaphore_signal(
                         barrier, inc=1, device_id={"space": other}, device_id_type=MESH
                     )
-
-    for brick in range(2):
-        other = 1 - brick
-        before = jnp.where(nb_ref[0, brick, 4] >= 0, 1.0, 0.0)
-        after = jnp.where(nb_ref[0, brick, 5] >= 0, 1.0, 0.0)
-        cz[brick, :, :, :ROWS] = c_ref[0, brick]
-        low = low_lanes((EDGE, EDGE, PAIR))
-        edge = jnp.where(
-            low,
-            c_ref[0, other, :, :, :PAIR].astype(jnp.float32) * after,
-            c_ref[0, other, :, :, ROWS - PAIR :].astype(jnp.float32) * before,
-        )
-        cz[brick, :, :, ROWS:] = edge.astype(jnp.bfloat16)
-    fys[0] = f_ref[0, 1].astype(jnp.float32)[:, EDGE - 1].astype(jnp.bfloat16)
-    fys[1] = f_ref[0, 0].astype(jnp.float32)[:, 0].astype(jnp.bfloat16)
-    cys[0] = cz[1].astype(jnp.float32)[:, EDGE - 1].astype(jnp.bfloat16)
-    cys[1] = cz[0].astype(jnp.float32)[:, 0].astype(jnp.bfloat16)
-
-    if reduce_here:
-        pl.semaphore_wait(barrier, count)
-    else:
-        for step in (1, 3, 4, 5):
-            for other in (me + step, me - step):
-
-                @pl.when(in_range(other, count))
-                def _():
-                    pl.semaphore_wait(barrier, 1)
 
     def halo(kind):
         x_ref, y_ref, ys_ref = ((fx, fy, fys), (cx, cy, cys))[kind]
@@ -194,10 +183,58 @@
         for _, arrives, copy in copies:
             pl.when(arrives)(copy.wait_recv)
 
+    loads[0].wait()
+    fys[0] = f_ref[0, 1].astype(jnp.float32)[:, EDGE - 1].astype(jnp.bfloat16)
+    fys[1] = f_ref[0, 0].astype(jnp.float32)[:, 0].astype(jnp.bfloat16)
+
+    if reduce_here:
+        pl.semaphore_wait(barrier, count)
+    else:
+        for step in (1, 3, 4, 5):
+            for other in (me + step, me - step):
+
+                @pl.when(in_range(other, count))
+                def _():
+                    pl.semaphore_wait(barrier, 1)
+
     f_copies, c_copies = halo(0), halo(1)
     start_halo(f_copies)
+
+    loads[1].wait()
+    loads[2].wait()
+    for brick in range(2):
+        other = 1 - brick
+        before = jnp.where(nb_ref[0, brick, 4] >= 0, 1.0, 0.0)
+        after = jnp.where(nb_ref[0, brick, 5] >= 0, 1.0, 0.0)
+        cz[brick, :, :, :ROWS] = c_ref[0, brick]
+        low = low_lanes((EDGE, EDGE, PAIR))
+        edge = jnp.where(
+            low,
+            c_ref[0, other, :, :, :PAIR].astype(jnp.float32) * after,
+            c_ref[0, other, :, :, ROWS - PAIR :].astype(jnp.float32) * before,
+        )
+        cz[brick, :, :, ROWS:] = edge.astype(jnp.bfloat16)
+    cys[0] = cz[1].astype(jnp.float32)[:, EDGE - 1].astype(jnp.bfloat16)
+    cys[1] = cz[0].astype(jnp.float32)[:, 0].astype(jnp.bfloat16)
     start_halo(c_copies)
 
+    cot_rows = []
+    zero_plane = jnp.zeros((EDGE, PAIR), jnp.float32)
+    for k in range(PAIRS):
+        per_tap = []
+        blocks = [
+            c_ref[0, brick, :, :, k * PAIR : (k + 1) * PAIR].astype(jnp.float32).reshape(EDGE * EDGE, PAIR)
+            for brick in range(2)
+        ]
+        for a in range(3):
+            pieces = []
+            for brick in range(2):
+                pieces += [zero_plane] * a + [blocks[brick]] + [zero_plane] * (2 - a)
+            per_tap.append(jnp.concatenate(pieces, axis=0))
+        cot_rows.append(jnp.concatenate(per_tap, axis=1))
+    ct[...] = jnp.concatenate(cot_rows, axis=0).T.astype(jnp.bfloat16)
+
+    loads[3].wait()
     order = (3, 0, 1, 2)
     blank = jnp.zeros((CH, CH), jnp.bfloat16)
     for a in range(3):
@@ -245,37 +282,23 @@
             )
         return jnp.concatenate(pieces, axis=0)
 
-    build_windows(
+    build_features = window_builder(
         xw, center, third_edge(center), row_low, row_high, third_edge(row_low), third_edge(row_high)
     )
 
-    cot_rows = []
-    zero_plane = jnp.zeros((EDGE, PAIR), jnp.float32)
-    for k in range(PAIRS):
-        per_tap = []
-        blocks = [
-            c_ref[0, brick, :, :, k * PAIR : (k + 1) * PAIR].astype(jnp.float32).reshape(EDGE * EDGE, PAIR)
-            for brick in range(2)
-        ]
-        for a in range(3):
-            pieces = []
-            for brick in range(2):
-                pieces += [zero_plane] * a + [blocks[brick]] + [zero_plane] * (2 - a)
-            per_tap.append(jnp.concatenate(pieces, axis=0))
-        cot_rows.append(jnp.concatenate(per_tap, axis=1).astype(jnp.bfloat16))
-    cot_all = jnp.concatenate(cot_rows, axis=0)
-    grad = lax.dot_general(
-        cot_all, xw[...], (((0,), (0,)), ((), ())), preferred_element_type=jnp.float32
-    )
     low = low_lanes((CH, PAIR))
     first_taps = []
-    for a in range(3):
-        for b in range(3):
-            cell0 = grad[a * PAIR : a * PAIR + CH, b * 4 * CH : (b + 1) * 4 * CH]
-            cell1 = grad[a * PAIR + CH : (a + 1) * PAIR, b * 4 * CH : (b + 1) * 4 * CH]
+    for b in range(3):
+        build_features(b)
+        grad = jnp.dot(
+            ct[...], xw[:, b * 4 * CH : (b + 1) * 4 * CH], preferred_element_type=jnp.float32
+        )
+        for a in range(3):
+            cell0 = grad[a * PAIR : a * PAIR + CH]
+            cell1 = grad[a * PAIR + CH : (a + 1) * PAIR]
             turned0 = pltpu.roll(cell1[:, :PAIR], CH, 1)
             turned1 = pltpu.roll(cell1[:, PAIR:], CH, 1)
-            part[a * 3 + b] = cell0[:, PAIR:] + jnp.where(low, turned1, turned0)
+            part[b * 3 + a] = cell0[:, PAIR:] + jnp.where(low, turned1, turned0)
             first_taps.append(cell0[:, :PAIR] + turned1)
     for m in range(5):
         high = first_taps[2 * m + 1] if 2 * m + 1 < 9 else jnp.zeros((CH, PAIR), jnp.float32)
@@ -289,12 +312,15 @@
         )
         core_copy.start()
 
-    result = jnp.dot(xw[...], wf[...], preferred_element_type=jnp.float32)
-
-    def put_response(brick, k, value):
-        resp_ref[0, brick, :, :, k * PAIR : (k + 1) * PAIR] = value
-
-    sum_taps(result, planes, put_response)
+    wait_halo(c_copies)
+    wide = stack([cz[b].astype(jnp.float32) for b in range(2)], cx, WIDE)
+    wide_low, wide_high = outer_rows(wide, cy, WIDE)
+    build_cotangent = window_builder(
+        cw, wide[..., :ROWS], wide[..., ROWS:], wide_low[..., :ROWS], wide_high[..., :ROWS],
+        wide_low[..., ROWS:], wide_high[..., ROWS:],
+    )
+    for tap in range(3):
+        build_cotangent(tap)
 
     if reduce_here:
         core_copy.wait()
@@ -316,13 +342,13 @@
             def _():
                 rbuf[tile] = sbuf[tile]
 
-    wait_halo(c_copies)
-    wide = stack([cz[b].astype(jnp.float32) for b in range(2)], cx, WIDE)
-    wide_low, wide_high = outer_rows(wide, cy, WIDE)
-    build_windows(
-        cw, wide[..., :ROWS], wide[..., ROWS:], wide_low[..., :ROWS], wide_high[..., :ROWS],
-        wide_low[..., ROWS:], wide_high[..., ROWS:],
-    )
+    result = jnp.dot(xw[...], wf[...], preferred_element_type=jnp.float32)
+
+    def put_response(brick, k, value):
+        resp_ref[0, brick, :, :, k * PAIR : (k + 1) * PAIR] = value
+
+    sum_taps(result, planes, put_response)
+
     result = lax.dot_general(
         cw[...], wg[...], (((1,), (1,)), ((), ())), preferred_element_type=jnp.float32
     )
@@ -331,17 +357,6 @@
         fg_ref[0, brick, :, :, k * PAIR : (k + 1) * PAIR] = value
 
     sum_taps(result, planes, put_gradient)
-
-    def finish(tile, value):
-        turned = (value * scale).T
-        if tile < 9:
-            kg_ref[tile // 3, tile % 3, 1] = turned[:CH]
-            kg_ref[tile // 3, tile % 3, 2] = turned[CH:]
-        else:
-            for half in range(2):
-                tap = 2 * (tile - 9) + half
-                if tap < 9:
-                    kg_ref[tap // 3, tap % 3, 0] = turned[half * CH : (half + 1) * CH]
 
     if reduce_here:
         for tile in range(OWNED):
@@ -401,8 +416,6 @@
                 send_sem=fw_send.at[tile], recv_sem=fw_recv.at[tile],
                 device_id={"dp": 1 - core}, device_id_type=MESH,
             ).wait_recv()
-        for tile in range(TILES):
-            finish(tile, fin[tile].astype(jnp.float32))
         for tile in range(OWNED):
             forward_copy(tile).wait_send()
 
@@ -410,11 +423,32 @@
         def _():
             for step in range(1, count):
                 gather_copy(step).wait_send()
-    else:
-        for tile in range(TILES):
-            finish(tile, part[tile])
     for sent, _, copy in f_copies + c_copies:
         pl.when(sent)(copy.wait_send)
+
+
+def finish_body(scale, resp_ref, fg_ref, tiles_ref, resp_hbm, fg_hbm, kg_hbm, kg, sems):
+    copies = [
+        pltpu.make_async_copy(resp_ref, resp_hbm, sems.at[0]),
+        pltpu.make_async_copy(fg_ref, fg_hbm, sems.at[1]),
+    ]
+    for copy in copies:
+        copy.start()
+    for tile in range(TILES):
+        turned = (tiles_ref[tile].astype(jnp.float32) * scale).T
+        for half in range(2):
+            block = turned[half * CH : (half + 1) * CH]
+            if tile < 9:
+                kg[tile % 3, tile // 3, half + 1] = block
+            else:
+                tap = 2 * (tile - 9) + half
+                if tap < 9:
+                    kg[tap % 3, tap // 3, 0] = block
+    last = pltpu.make_async_copy(kg, kg_hbm, sems.at[2])
+    last.start()
+    for copy in copies:
+        copy.wait()
+    last.wait()
 
 
 def body(features, cotangent, kernel, neighbours):
@@ -428,16 +462,22 @@
     rows = PAIRS * planes * EDGE
     dma = pltpu.SemaphoreType.DMA
     vmem = pl.BlockSpec(memory_space=pltpu.VMEM)
-    response, feature_grad, kernel_grad = pl.pallas_call(
-        functools.partial(kernel_body, count, dp_count, scale, reduce_here),
+    hbm = pl.BlockSpec(memory_space=pltpu.HBM)
+    part_shape = (TILES, CH, PAIR)
+    response, feature_grad, tiles = pl.pallas_call(
+        functools.partial(kernel_body, count, reduce_here),
         out_shape=(
             jax.ShapeDtypeStruct(features.shape, bf16),
             jax.ShapeDtypeStruct(features.shape, bf16),
-            jax.ShapeDtypeStruct(kernel.shape, f32),
+            jax.ShapeDtypeStruct(part_shape, bf16 if reduce_here else f32),
         ),
-        in_specs=[pl.BlockSpec(memory_space=pltpu.SMEM), vmem, vmem, vmem],
+        in_specs=[hbm] * 4,
         out_specs=(vmem, vmem, vmem),
         scratch_shapes=[
+            pltpu.SMEM(neighbours.shape, jnp.int32),
+            pltpu.VMEM(features.shape, bf16),
+            pltpu.VMEM(features.shape, bf16),
+            pltpu.VMEM(kernel.shape, bf16),
             pltpu.VMEM((2, 2, EDGE, ROWS), bf16),
             pltpu.VMEM((2, 3, EDGE, ROWS), bf16),
             pltpu.VMEM((2, 2, EDGE, WIDE), bf16),
@@ -447,24 +487,38 @@
             pltpu.VMEM((2, EDGE, EDGE, WIDE), bf16),
             pltpu.VMEM((rows, 12 * CH), bf16),
             pltpu.VMEM((rows, 12 * CH), bf16),
+            pltpu.VMEM((6 * CH, rows), bf16),
             pltpu.VMEM((12 * CH, 6 * CH), bf16),
             pltpu.VMEM((6 * CH, 12 * CH), bf16),
-            pltpu.VMEM((TILES, CH, PAIR), f32),
+            pltpu.VMEM(part_shape, f32),
             pltpu.VMEM((OWNED, CH, PAIR), f32),
             pltpu.VMEM((OWNED, CH, PAIR), bf16),
             pltpu.VMEM((8, CH, PAIR), bf16),
-            pltpu.VMEM((TILES, CH, PAIR), bf16),
-            dma((16,)), dma((16,)), dma((2,)), dma((8,)), dma((8,)),
+            dma((4,)), dma((16,)), dma((16,)), dma((2,)), dma((8,)), dma((8,)),
             dma((8,)), dma((8,)), dma((8,)), dma((8,)),
         ],
         compiler_params=pltpu.CompilerParams(
             collective_id=0, has_side_effects=True, vmem_limit_bytes=40 * 1024 * 1024
         ),
         cost_estimate=pl.CostEstimate(flops=10**9, bytes_accessed=2 * 10**6, transcendentals=0),
-    )(neighbours, features, cotangent, kernel)
+    )(*(
+        pltpu.with_memory_space_constraint(x, pltpu.HBM)
+        for x in (neighbours, features, cotangent, kernel)
+    ))
     if not reduce_here:
-        kernel_grad = lax.psum(kernel_grad, ("space", "dp"))
-    return (response, feature_grad, kernel_grad)
+        tiles = lax.psum(tiles, ("space", "dp"))
+    return pl.pallas_call(
+        functools.partial(finish_body, scale),
+        out_shape=(
+            jax.ShapeDtypeStruct(features.shape, bf16),
+            jax.ShapeDtypeStruct(features.shape, bf16),
+            jax.ShapeDtypeStruct(kernel.shape, f32),
+        ),
+        in_specs=[vmem] * 3,
+        out_specs=(hbm,) * 3,
+        scratch_shapes=[pltpu.VMEM(kernel.shape, f32), dma((3,))],
+        cost_estimate=pl.CostEstimate(flops=10**6, bytes_accessed=10**6, transcendentals=0),
+    )(response, feature_grad, tiles)
 
 
 def solution(mesh):

time: 29.9 us -> 27.7 us (0.926)
  local copies, waits for them, and re-layouts: 5.72 us -> 1.96 us
  Pallas kernels: 23.1 us -> 24.9 us
    unnamed x11 -> x6, local copies, waits for them, and re-layouts: 5.72 us -> 1.96 us
    pallas_call x1 -> x2, Pallas kernels: 23.1 us -> 24.9 us  [the longest x1 22.6 us: body(): pl.pallas_call(functools.partial(kernel_body, count, reduce_here), out_sh...]
where the time goes in v2:
time: 27.7 us; the launch traced here: 27.5 us
  Pallas kernels  24.9 us (90%)
  local copies, waits for them, and re-layouts  1.96 us (7%)
  between operations  0.65 us (2%)
    pallas_call x1, Pallas kernels, body(): pl.pallas_call(functools.partial(kernel_body, count, reduce_here), out_sh...  22.6 us
    pallas_call x1, Pallas kernels, body(): pl.pallas_call(functools.partial(finish_body, scale), out_shape=(jax.Shap...  2.31 us
    unnamed x6, local copies, waits for them, and re-layouts  1.96 us

profile of v2, /device:TPU:0, one launch (start us, length us, event | category | flops | bytes accessed | tf_op | source)
XLA Modules:
  0.0 27.5 jit_solution(9617696367323062494)
XLA Ops:
  0.6 22.6 %shard_map.67 = (bf16[1,2,8,8,512]{4,3,2,1,0:T(8,128)(2,1)S(1)}, bf16[1,2,8,8,512]{4,3,2,1,0:T(8,128)(2,1)S(1)}, bf16[14,64,128]{2,1,0:T(8,128)(2,1)S(1)}) custom-call(s32[1,2,6]{2,1,0:T(2,128)} %nb_hbm.1, bf16[1,2,8,8,512]{4,3,2,1,0:T(8,128)(2,1)} %f_hbm.1, bf16[1,2,8,8,512]{4,3,2,1,0:T(8,128)(2,1)} %c_hbm.1, bf16[3,3,3,64,64]{4,3,2,1,0:T(8,128)(2,1)} %w_hbm.1), custom_call_target="tpu_custom_call" | custom-call | flops 1000000000 | bytes 2000000 | tf_op jit(solution)/shard_map/pallas_call | solution.py:467
  23.2 0.0 copy-start
  23.2 0.7 %copy-done = bf16[14,64,128]{2,1,0:T(8,128)(2,1)} copy-done((bf16[14,64,128]{2,1,0:T(8,128)(2,1)}, bf16[14,64,128]{2,1,0:T(8,128)(2,1)S(1)}, u32[]{:S(2)}) %copy-start) | copy-done | bytes 229400
  23.9 0.0 copy-start.1
  23.9 0.7 %copy-done.1 = bf16[1,2,8,8,512]{4,3,2,1,0:T(8,128)(2,1)} copy-done((bf16[1,2,8,8,512]{4,3,2,1,0:T(8,128)(2,1)}, bf16[1,2,8,8,512]{4,3,2,1,0:T(8,128)(2,1)S(1)}, u32[]{:S(2)}) %copy-start.1) | copy-done | bytes 131096
  24.6 0.0 copy-start.2
  24.6 0.6 %copy-done.2 = bf16[1,2,8,8,512]{4,3,2,1,0:T(8,128)(2,1)} copy-done((bf16[1,2,8,8,512]{4,3,2,1,0:T(8,128)(2,1)}, bf16[1,2,8,8,512]{4,3,2,1,0:T(8,128)(2,1)S(1)}, u32[]{:S(2)}) %copy-start.2) | copy-done | bytes 131096
  25.2 2.3 %shard_map.68 = (bf16[1,2,8,8,512]{4,3,2,1,0:T(8,128)(2,1)}, bf16[1,2,8,8,512]{4,3,2,1,0:T(8,128)(2,1)}, f32[3,3,3,64,64]{4,3,2,1,0:T(8,128)}) custom-call(bf16[1,2,8,8,512]{4,3,2,1,0:T(8,128)(2,1)} %copy-done.1, bf16[1,2,8,8,512]{4,3,2,1,0:T(8,128)(2,1)} %copy-done.2, bf16[14,64,128]{2,1,0:T(8,128)(2,1)} %copy-done), custom_call_target="tpu_custom_call" | custom-call | flops 1000000 | bytes 1000000 | tf_op jit(solution)/shard_map/pallas_call | solution.py:510
Async XLA Ops:
  23.2 0.7 %copy-start = (bf16[14,64,128]{2,1,0:T(8,128)(2,1)}, bf16[14,64,128]{2,1,0:T(8,128)(2,1)S(1)}, u32[]{:S(2)}) copy-start(bf16[14,64,128]{2,1,0:T(8,128)(2,1)S(1)} %get-tuple-element.8.tiles_ref) | copy-start | bytes 688132
  23.9 0.7 %copy-start.1 = (bf16[1,2,8,8,512]{4,3,2,1,0:T(8,128)(2,1)}, bf16[1,2,8,8,512]{4,3,2,1,0:T(8,128)(2,1)S(1)}, u32[]{:S(2)}) copy-start(bf16[1,2,8,8,512]{4,3,2,1,0:T(8,128)(2,1)S(1)} %get-tuple-element.6.resp_ref) | copy-start | bytes 393220
  24.6 0.6 %copy-start.2 = (bf16[1,2,8,8,512]{4,3,2,1,0:T(8,128)(2,1)}, bf16[1,2,8,8,512]{4,3,2,1,0:T(8,128)(2,1)S(1)}, u32[]{:S(2)}) copy-start(bf16[1,2,8,8,512]{4,3,2,1,0:T(8,128)(2,1)S(1)} %get-tuple-element.7.fg_ref) | copy-start | bytes 393220

commit v3 on v2

--- a/solution.py
+++ b/solution.py
@@ -95,6 +95,11 @@
                 start = base + a * EDGE
                 total = total + result[start : start + EDGE * EDGE, a * PAIR : (a + 1) * PAIR]
             store(brick, k, total.reshape(EDGE, EDGE, PAIR).astype(jnp.bfloat16))
+
+
+def turn(tile):
+    turned = tile.T
+    return jnp.concatenate([turned[:CH], turned[CH:]], axis=1)
 
 
 def kernel_body(
@@ -234,6 +239,62 @@
         cot_rows.append(jnp.concatenate(per_tap, axis=1))
     ct[...] = jnp.concatenate(cot_rows, axis=0).T.astype(jnp.bfloat16)
 
+    wait_halo(f_copies)
+
+    def stack(values, x_ref, width):
+        parts = []
+        for brick in range(2):
+            parts.append(x_ref[0, brick].astype(jnp.float32)[None, :, :width])
+            parts.append(values[brick])
+            parts.append(x_ref[1, brick].astype(jnp.float32)[None, :, :width])
+        return jnp.concatenate(parts, axis=0)
+
+    center = stack([f_ref[0, b].astype(jnp.float32) for b in range(2)], fx, ROWS)
+    row_low, row_high = outer_rows(center, fy, ROWS)
+
+    def third_edge(values):
+        pieces = []
+        half = planes // 2
+        for brick in range(2):
+            other = values[(1 - brick) * half : (2 - brick) * half]
+            before = jnp.where(nb_ref[0, brick, 4] >= 0, 1.0, 0.0)
+            after = jnp.where(nb_ref[0, brick, 5] >= 0, 1.0, 0.0)
+            low = low_lanes((half, values.shape[1], PAIR))
+            pieces.append(
+                jnp.where(low, other[..., :PAIR] * after, other[..., ROWS - PAIR :] * before)
+            )
+        return jnp.concatenate(pieces, axis=0)
+
+    build_features = window_builder(
+        xw, center, third_edge(center), row_low, row_high, third_edge(row_low), third_edge(row_high)
+    )
+
+    low = low_lanes((CH, PAIR))
+    first_taps = []
+    for b in range(3):
+        build_features(b)
+        grad = jnp.dot(
+            ct[...], xw[:, b * 4 * CH : (b + 1) * 4 * CH], preferred_element_type=jnp.float32
+        )
+        for a in range(3):
+            cell0 = grad[a * PAIR : a * PAIR + CH]
+            cell1 = grad[a * PAIR + CH : (a + 1) * PAIR]
+            turned0 = pltpu.roll(cell1[:, :PAIR], CH, 1)
+            turned1 = pltpu.roll(cell1[:, PAIR:], CH, 1)
+            part[b * 3 + a] = cell0[:, PAIR:] + jnp.where(low, turned1, turned0)
+            first_taps.append(cell0[:, :PAIR] + turned1)
+    for m in range(5):
+        high = first_taps[2 * m + 1] if 2 * m + 1 < 9 else jnp.zeros((CH, PAIR), jnp.float32)
+        part[9 + m] = jnp.where(low, pltpu.roll(first_taps[2 * m], CH, 1), high)
+
+    if reduce_here:
+        core_copy = pltpu.make_async_remote_copy(
+            src_ref=part.at[pl.ds((1 - core) * OWNED, OWNED)], dst_ref=core_in,
+            send_sem=core_sem.at[0], recv_sem=core_sem.at[1],
+            device_id={"dp": 1 - core}, device_id_type=MESH,
+        )
+        core_copy.start()
+
     loads[3].wait()
     order = (3, 0, 1, 2)
     blank = jnp.zeros((CH, CH), jnp.bfloat16)
@@ -256,61 +317,33 @@
                     lane = flip_b * 4 * CH + half * PAIR
                     wg[row : row + CH, lane : lane + PAIR] = jnp.concatenate(pieces, axis=1)
 
-    wait_halo(f_copies)
-
-    def stack(values, x_ref, width):
-        parts = []
-        for brick in range(2):
-            parts.append(x_ref[0, brick].astype(jnp.float32)[None, :, :width])
-            parts.append(values[brick])
-            parts.append(x_ref[1, brick].astype(jnp.float32)[None, :, :width])
-        return jnp.concatenate(parts, axis=0)
-
-    center = stack([f_ref[0, b].astype(jnp.float32) for b in range(2)], fx, ROWS)
-    row_low, row_high = outer_rows(center, fy, ROWS)
-
-    def third_edge(values):
-        pieces = []
-        half = planes // 2
-        for brick in range(2):
-            other = values[(1 - brick) * half : (2 - brick) * half]
-            before = jnp.where(nb_ref[0, brick, 4] >= 0, 1.0, 0.0)
-            after = jnp.where(nb_ref[0, brick, 5] >= 0, 1.0, 0.0)
-            low = low_lanes((half, values.shape[1], PAIR))
-            pieces.append(
-                jnp.where(low, other[..., :PAIR] * after, other[..., ROWS - PAIR :] * before)
+    if reduce_here:
+        core_copy.wait()
+        for tile in range(OWNED):
+            sbuf[tile] = (part[core * OWNED + tile] + core_in[tile]).astype(jnp.bfloat16)
+
+        def scatter_copy(step):
+            target = (me + step) % count
+            return target, pltpu.make_async_remote_copy(
+                src_ref=sbuf.at[target], dst_ref=rbuf.at[me],
+                send_sem=rs_send.at[step], recv_sem=rs_recv.at[me],
+                device_id={"space": target}, device_id_type=MESH,
             )
-        return jnp.concatenate(pieces, axis=0)
-
-    build_features = window_builder(
-        xw, center, third_edge(center), row_low, row_high, third_edge(row_low), third_edge(row_high)
-    )
-
-    low = low_lanes((CH, PAIR))
-    first_taps = []
-    for b in range(3):
-        build_features(b)
-        grad = jnp.dot(
-            ct[...], xw[:, b * 4 * CH : (b + 1) * 4 * CH], preferred_element_type=jnp.float32
-        )
-        for a in range(3):
-            cell0 = grad[a * PAIR : a * PAIR + CH]
-            cell1 = grad[a * PAIR + CH : (a + 1) * PAIR]
-            turned0 = pltpu.roll(cell1[:, :PAIR], CH, 1)
-            turned1 = pltpu.roll(cell1[:, PAIR:], CH, 1)
-            part[b * 3 + a] = cell0[:, PAIR:] + jnp.where(low, turned1, turned0)
-            first_taps.append(cell0[:, :PAIR] + turned1)
-    for m in range(5):
-        high = first_taps[2 * m + 1] if 2 * m + 1 < 9 else jnp.zeros((CH, PAIR), jnp.float32)
-        part[9 + m] = jnp.where(low, pltpu.roll(first_taps[2 * m], CH, 1), high)
-
-    if reduce_here:
-        core_copy = pltpu.make_async_remote_copy(
-            src_ref=part.at[pl.ds((1 - core) * OWNED, OWNED)], dst_ref=core_in,
-            send_sem=core_sem.at[0], recv_sem=core_sem.at[1],
-            device_id={"dp": 1 - core}, device_id_type=MESH,
-        )
-        core_copy.start()
+
+        for step in range(1, count):
+            target, copy = scatter_copy(step)
+            pl.when(target < OWNED)(copy.start)
+
+        @pl.when(me < OWNED)
+        def _():
+            rbuf[me] = sbuf[me]
+
+    result = jnp.dot(xw[...], wf[...], preferred_element_type=jnp.float32)
+
+    def put_response(brick, k, value):
+        resp_ref[0, brick, :, :, k * PAIR : (k + 1) * PAIR] = value
+
+    sum_taps(result, planes, put_response)
 
     wait_halo(c_copies)
     wide = stack([cz[b].astype(jnp.float32) for b in range(2)], cx, WIDE)
@@ -323,44 +356,9 @@
         build_cotangent(tap)
 
     if reduce_here:
-        core_copy.wait()
-        rs_copies = []
-        for tile in range(OWNED):
-            sbuf[tile] = (part[core * OWNED + tile] + core_in[tile]).astype(jnp.bfloat16)
-            copy = pltpu.make_async_remote_copy(
-                src_ref=sbuf.at[tile], dst_ref=rbuf.at[me],
-                send_sem=rs_send.at[tile], recv_sem=rs_recv.at[me],
-                device_id={"space": tile}, device_id_type=MESH,
-            )
-            rs_copies.append(copy)
-
-            @pl.when(me != tile)
-            def _():
-                copy.start()
-
-            @pl.when(me == tile)
-            def _():
-                rbuf[tile] = sbuf[tile]
-
-    result = jnp.dot(xw[...], wf[...], preferred_element_type=jnp.float32)
-
-    def put_response(brick, k, value):
-        resp_ref[0, brick, :, :, k * PAIR : (k + 1) * PAIR] = value
-
-    sum_taps(result, planes, put_response)
-
-    result = lax.dot_general(
-        cw[...], wg[...], (((1,), (1,)), ((), ())), preferred_element_type=jnp.float32
-    )
-
-    def put_gradient(brick, k, value):
-        fg_ref[0, brick, :, :, k * PAIR : (k + 1) * PAIR] = value
-
-    sum_taps(result, planes, put_gradient)
-
-    if reduce_here:
-        for tile in range(OWNED):
-            pl.when(me != tile)(rs_copies[tile].wait_send)
+        for step in range(1, count):
+            target, copy = scatter_copy(step)
+            pl.when(target < OWNED)(copy.wait_send)
 
         def gather_copy(step):
             target = (me + step) % count
@@ -392,10 +390,20 @@
                     ).wait_recv()
 
                 total = total + rbuf[source].astype(jnp.float32)
-            fin[core * OWNED + me] = total.astype(jnp.bfloat16)
+            fin[core * OWNED + me] = turn(total).astype(jnp.bfloat16)
             for step in range(1, count):
                 gather_copy(step).start()
 
+    result = lax.dot_general(
+        cw[...], wg[...], (((1,), (1,)), ((), ())), preferred_element_type=jnp.float32
+    )
+
+    def put_gradient(brick, k, value):
+        fg_ref[0, brick, :, :, k * PAIR : (k + 1) * PAIR] = value
+
+    sum_taps(result, planes, put_gradient)
+
+    if reduce_here:
         for tile in range(OWNED):
 
             @pl.when(me != tile)
@@ -423,6 +431,9 @@
         def _():
             for step in range(1, count):
                 gather_copy(step).wait_send()
+    else:
+        for tile in range(TILES):
+            part[tile] = turn(part[tile])
     for sent, _, copy in f_copies + c_copies:
         pl.when(sent)(copy.wait_send)
 
@@ -434,21 +445,18 @@
     ]
     for copy in copies:
         copy.start()
-    for tile in range(TILES):
-        turned = (tiles_ref[tile].astype(jnp.float32) * scale).T
-        for half in range(2):
-            block = turned[half * CH : (half + 1) * CH]
-            if tile < 9:
-                kg[tile % 3, tile // 3, half + 1] = block
-            else:
-                tap = 2 * (tile - 9) + half
-                if tap < 9:
-                    kg[tap % 3, tap // 3, 0] = block
-    last = pltpu.make_async_copy(kg, kg_hbm, sems.at[2])
-    last.start()
+    for a in range(3):
+        for b in range(3):
+            tap = b * 3 + a
+            later = tiles_ref[tap].astype(jnp.float32) * scale
+            first = tiles_ref[9 + tap // 2].astype(jnp.float32) * scale
+            kg[a, b, 0] = first[:, tap % 2 * CH : (tap % 2 + 1) * CH]
+            kg[a, b, 1] = later[:, :CH]
+            kg[a, b, 2] = later[:, CH:]
+        copies.append(pltpu.make_async_copy(kg.at[a], kg_hbm.at[a], sems.at[2 + a]))
+        copies[-1].start()
     for copy in copies:
         copy.wait()
-    last.wait()
 
 
 def body(features, cotangent, kernel, neighbours):
@@ -467,9 +475,9 @@
     response, feature_grad, tiles = pl.pallas_call(
         functools.partial(kernel_body, count, reduce_here),
         out_shape=(
-            jax.ShapeDtypeStruct(features.shape, bf16),
-            jax.ShapeDtypeStruct(features.shape, bf16),
-            jax.ShapeDtypeStruct(part_shape, bf16 if reduce_here else f32),
+            pltpu.VMEM(features.shape, bf16),
+            pltpu.VMEM(features.shape, bf16),
+            pltpu.VMEM(part_shape, bf16 if reduce_here else f32),
         ),
         in_specs=[hbm] * 4,
         out_specs=(vmem, vmem, vmem),
@@ -492,7 +500,7 @@
             pltpu.VMEM((6 * CH, 12 * CH), bf16),
             pltpu.VMEM(part_shape, f32),
             pltpu.VMEM((OWNED, CH, PAIR), f32),
-            pltpu.VMEM((OWNED, CH, PAIR), bf16),
+            pltpu.VMEM((8, CH, PAIR), bf16),
             pltpu.VMEM((8, CH, PAIR), bf16),
             dma((4,)), dma((16,)), dma((16,)), dma((2,)), dma((8,)), dma((8,)),
             dma((8,)), dma((8,)), dma((8,)), dma((8,)),
@@ -516,9 +524,12 @@
         ),
         in_specs=[vmem] * 3,
         out_specs=(hbm,) * 3,
-        scratch_shapes=[pltpu.VMEM(kernel.shape, f32), dma((3,))],
+        scratch_shapes=[pltpu.VMEM(kernel.shape, f32), dma((5,))],
         cost_estimate=pl.CostEstimate(flops=10**6, bytes_accessed=10**6, transcendentals=0),
-    )(response, feature_grad, tiles)
+    )(*(
+        pltpu.with_memory_space_constraint(x, pltpu.VMEM)
+        for x in (response, feature_grad, tiles)
+    ))
 
 
 def solution(mesh):

time: 27.7 us -> 24.6 us (0.89)
  local copies, waits for them, and re-layouts: 1.96 us -> 0 us
  Pallas kernels: 24.9 us -> 23.8 us
    unnamed x6 -> x0, local copies, waits for them, and re-layouts: 1.96 us -> none
    pallas_call x1, Pallas kernels: 2.31 us -> 1.06 us  [body(): pl.pallas_call(functools.partial(finish_body, scale), out_shape=(jax.Shap...]
where the time goes in v3:
time: 24.6 us; the launch traced here: 24.4 us
  Pallas kernels  23.8 us (97%)
  between operations  0.64 us (3%)
    pallas_call x1, Pallas kernels, body(): pl.pallas_call(functools.partial(kernel_body, count, reduce_here), out_sh...  22.8 us
    pallas_call x1, Pallas kernels, body(): pl.pallas_call(functools.partial(finish_body, scale), out_shape=(jax.Shap...  1.06 us

profile of v3, /device:TPU:0, one launch (start us, length us, event | category | flops | bytes accessed | tf_op | source)
XLA Modules:
  0.0 24.4 jit_solution(6542163768472375240)
XLA Ops:
  0.6 22.8 %shard_map.67 = (bf16[1,2,8,8,512]{4,3,2,1,0:T(8,128)(2,1)S(1)}, bf16[1,2,8,8,512]{4,3,2,1,0:T(8,128)(2,1)S(1)}, bf16[14,64,128]{2,1,0:T(8,128)(2,1)S(1)}) custom-call(s32[1,2,6]{2,1,0:T(2,128)} %nb_hbm.1, bf16[1,2,8,8,512]{4,3,2,1,0:T(8,128)(2,1)} %f_hbm.1, bf16[1,2,8,8,512]{4,3,2,1,0:T(8,128)(2,1)} %c_hbm.1, bf16[3,3,3,64,64]{4,3,2,1,0:T(8,128)(2,1)} %w_hbm.1), custom_call_target="tpu_custom_call" | custom-call | flops 1000000000 | bytes 2000000 | tf_op jit(solution)/shard_map/pallas_call | solution.py:475
  23.4 1.1 %shard_map.68 = (bf16[1,2,8,8,512]{4,3,2,1,0:T(8,128)(2,1)}, bf16[1,2,8,8,512]{4,3,2,1,0:T(8,128)(2,1)}, f32[3,3,3,64,64]{4,3,2,1,0:T(8,128)}) custom-call(bf16[1,2,8,8,512]{4,3,2,1,0:T(8,128)(2,1)S(1)} %get-tuple-element.6.resp_ref, bf16[1,2,8,8,512]{4,3,2,1,0:T(8,128)(2,1)S(1)} %get-tuple-element.7.fg_ref, bf16[14,64,128]{2,1,0:T(8,128)(2,1)S(1)} %get-tuple-element.8.tiles_ref), custom_call_target="tpu_custom_call" | custom-call | flops 1000000 | bytes 1000000 | tf_op jit(solution)/shard_map/pallas_call | solution.py:518

commit v4 on v3

--- a/solution.py
+++ b/solution.py
@@ -18,6 +18,13 @@
 TILES = 14
 OWNED = TILES // 2
 MESH = pl.DeviceIdType.MESH
+BATCHES = ((0, 2), (2, 4), (4, 7))
+READY = (
+    [("late", 0), ("late", 1), ("late", 2), ("early", 0)]
+    + [("late", 3), ("late", 4), ("late", 5), ("early", 1)]
+    + [("early", 2), ("late", 6), ("late", 7), ("late", 8), ("early", 3), ("early", 4)]
+)
+SPOT = {name: number % 2 * OWNED + number // 2 for number, name in enumerate(READY)}
 DIAGONALS = [(side, dx) for side in range(2) for dx in range(3)]
 
 
@@ -108,7 +115,7 @@
     resp_ref, fg_ref, tiles_ref,
     nb_ref, f_ref, c_ref, w_ref,
     fx, fy, cx, cy, fys, cys, cz, xw, cw, ct, wf, wg, part, core_in, sbuf, rbuf,
-    load_sem, halo_send, halo_recv, core_sem, rs_send, rs_recv, ag_send, ag_recv, fw_send, fw_recv,
+    load_sem, halo_send, halo_recv, core_send, core_recv, rs_send, rs_recv, ag_send, ag_recv, fw_send, fw_recv,
 ):
     me = lax.axis_index("space")
     core = lax.axis_index("dp")
@@ -270,6 +277,30 @@
     )
 
     low = low_lanes((CH, PAIR))
+    core_copies = [
+        pltpu.make_async_remote_copy(
+            src_ref=part.at[pl.ds((1 - core) * OWNED + first, last - first)],
+            dst_ref=core_in.at[pl.ds(first, last - first)],
+            send_sem=core_send.at[batch], recv_sem=core_recv.at[batch],
+            device_id={"dp": 1 - core}, device_id_type=MESH,
+        )
+        for batch, (first, last) in enumerate(BATCHES)
+    ] if reduce_here else []
+
+    def scatter_copy(tile):
+        return pltpu.make_async_remote_copy(
+            src_ref=sbuf.at[tile], dst_ref=rbuf.at[me],
+            send_sem=rs_send.at[tile], recv_sem=rs_recv.at[me],
+            device_id={"space": tile}, device_id_type=MESH,
+        )
+
+    def scatter(batch):
+        core_copies[batch].wait_recv()
+        for tile in range(*BATCHES[batch]):
+            total = part[core * OWNED + tile] + core_in[tile]
+            sbuf[tile] = total.astype(jnp.bfloat16)
+            pl.when(me != tile)(scatter_copy(tile).start)
+
     first_taps = []
     for b in range(3):
         build_features(b)
@@ -281,19 +312,16 @@
             cell1 = grad[a * PAIR + CH : (a + 1) * PAIR]
             turned0 = pltpu.roll(cell1[:, :PAIR], CH, 1)
             turned1 = pltpu.roll(cell1[:, PAIR:], CH, 1)
-            part[b * 3 + a] = cell0[:, PAIR:] + jnp.where(low, turned1, turned0)
+            tap = b * 3 + a
+            part[SPOT["late", tap]] = cell0[:, PAIR:] + jnp.where(low, turned1, turned0)
             first_taps.append(cell0[:, :PAIR] + turned1)
-    for m in range(5):
-        high = first_taps[2 * m + 1] if 2 * m + 1 < 9 else jnp.zeros((CH, PAIR), jnp.float32)
-        part[9 + m] = jnp.where(low, pltpu.roll(first_taps[2 * m], CH, 1), high)
-
-    if reduce_here:
-        core_copy = pltpu.make_async_remote_copy(
-            src_ref=part.at[pl.ds((1 - core) * OWNED, OWNED)], dst_ref=core_in,
-            send_sem=core_sem.at[0], recv_sem=core_sem.at[1],
-            device_id={"dp": 1 - core}, device_id_type=MESH,
-        )
-        core_copy.start()
+            if tap % 2 == 1 or tap == 8:
+                pair = first_taps[tap - tap % 2 :] + [jnp.zeros((CH, PAIR), jnp.float32)]
+                part[SPOT["early", tap // 2]] = jnp.where(low, pltpu.roll(pair[0], CH, 1), pair[1])
+        if reduce_here:
+            core_copies[b].start()
+            if b > 0:
+                scatter(b - 1)
 
     loads[3].wait()
     order = (3, 0, 1, 2)
@@ -318,21 +346,7 @@
                     wg[row : row + CH, lane : lane + PAIR] = jnp.concatenate(pieces, axis=1)
 
     if reduce_here:
-        core_copy.wait()
-        for tile in range(OWNED):
-            sbuf[tile] = (part[core * OWNED + tile] + core_in[tile]).astype(jnp.bfloat16)
-
-        def scatter_copy(step):
-            target = (me + step) % count
-            return target, pltpu.make_async_remote_copy(
-                src_ref=sbuf.at[target], dst_ref=rbuf.at[me],
-                send_sem=rs_send.at[step], recv_sem=rs_recv.at[me],
-                device_id={"space": target}, device_id_type=MESH,
-            )
-
-        for step in range(1, count):
-            target, copy = scatter_copy(step)
-            pl.when(target < OWNED)(copy.start)
+        scatter(2)
 
         @pl.when(me < OWNED)
         def _():
@@ -356,10 +370,6 @@
         build_cotangent(tap)
 
     if reduce_here:
-        for step in range(1, count):
-            target, copy = scatter_copy(step)
-            pl.when(target < OWNED)(copy.wait_send)
-
         def gather_copy(step):
             target = (me + step) % count
             return pltpu.make_async_remote_copy(
@@ -434,6 +444,11 @@
     else:
         for tile in range(TILES):
             part[tile] = turn(part[tile])
+    if reduce_here:
+        for copy in core_copies:
+            copy.wait_send()
+        for tile in range(OWNED):
+            pl.when(me != tile)(scatter_copy(tile).wait_send)
     for sent, _, copy in f_copies + c_copies:
         pl.when(sent)(copy.wait_send)
 
@@ -448,8 +463,8 @@
     for a in range(3):
         for b in range(3):
             tap = b * 3 + a
-            later = tiles_ref[tap].astype(jnp.float32) * scale
-            first = tiles_ref[9 + tap // 2].astype(jnp.float32) * scale
+            later = tiles_ref[SPOT["late", tap]].astype(jnp.float32) * scale
+            first = tiles_ref[SPOT["early", tap // 2]].astype(jnp.float32) * scale
             kg[a, b, 0] = first[:, tap % 2 * CH : (tap % 2 + 1) * CH]
             kg[a, b, 1] = later[:, :CH]
             kg[a, b, 2] = later[:, CH:]
@@ -502,7 +517,7 @@
             pltpu.VMEM((OWNED, CH, PAIR), f32),
             pltpu.VMEM((8, CH, PAIR), bf16),
             pltpu.VMEM((8, CH, PAIR), bf16),
-            dma((4,)), dma((16,)), dma((16,)), dma((2,)), dma((8,)), dma((8,)),
+            dma((4,)), dma((16,)), dma((16,)), dma((3,)), dma((3,)), dma((8,)), dma((8,)),
             dma((8,)), dma((8,)), dma((8,)), dma((8,)),
         ],
         compiler_params=pltpu.CompilerParams(

time: 24.6 us -> 25.1 us (1.020)
  Pallas kernels: 23.8 us -> 24.3 us
    pallas_call x1, Pallas kernels: 22.8 us -> 23.3 us  [body(): pl.pallas_call(functools.partial(kernel_body, count, reduce_here), out_sh...]
where the time goes in v4:
time: 25.1 us; the launch traced here: 25 us
  Pallas kernels  24.3 us (97%)
  between operations  0.64 us (3%)
    pallas_call x1, Pallas kernels, body(): pl.pallas_call(functools.partial(kernel_body, count, reduce_here), out_sh...  23.3 us
    pallas_call x1, Pallas kernels, body(): pl.pallas_call(functools.partial(finish_body, scale), out_shape=(jax.Shap...  1.06 us

profile of v4, /device:TPU:0, one launch (start us, length us, event | category | flops | bytes accessed | tf_op | source)
XLA Modules:
  0.0 25.0 jit_solution(5326641453532593190)
XLA Ops:
  0.6 23.3 %shard_map.67 = (bf16[1,2,8,8,512]{4,3,2,1,0:T(8,128)(2,1)S(1)}, bf16[1,2,8,8,512]{4,3,2,1,0:T(8,128)(2,1)S(1)}, bf16[14,64,128]{2,1,0:T(8,128)(2,1)S(1)}) custom-call(s32[1,2,6]{2,1,0:T(2,128)} %nb_hbm.1, bf16[1,2,8,8,512]{4,3,2,1,0:T(8,128)(2,1)} %f_hbm.1, bf16[1,2,8,8,512]{4,3,2,1,0:T(8,128)(2,1)} %c_hbm.1, bf16[3,3,3,64,64]{4,3,2,1,0:T(8,128)(2,1)} %w_hbm.1), custom_call_target="tpu_custom_call" | custom-call | flops 1000000000 | bytes 2000000 | tf_op jit(solution)/shard_map/pallas_call | solution.py:490
  23.9 1.1 %shard_map.68 = (bf16[1,2,8,8,512]{4,3,2,1,0:T(8,128)(2,1)}, bf16[1,2,8,8,512]{4,3,2,1,0:T(8,128)(2,1)}, f32[3,3,3,64,64]{4,3,2,1,0:T(8,128)}) custom-call(bf16[1,2,8,8,512]{4,3,2,1,0:T(8,128)(2,1)S(1)} %get-tuple-element.6.resp_ref, bf16[1,2,8,8,512]{4,3,2,1,0:T(8,128)(2,1)S(1)} %get-tuple-element.7.fg_ref, bf16[14,64,128]{2,1,0:T(8,128)(2,1)S(1)} %get-tuple-element.8.tiles_ref), custom_call_target="tpu_custom_call" | custom-call | flops 1000000 | bytes 1000000 | tf_op jit(solution)/shard_map/pallas_call | solution.py:533

commit v5 on v4

--- a/solution.py
+++ b/solution.py
@@ -43,65 +43,54 @@
     return in_range(tile, count) & in_range(between, count) & there
 
 
-def place_windows(store, center, edge):
-    low = low_lanes((center.shape[0], PAIR))
-    pairs = [center[:, PAIR * k : PAIR * (k + 1)] for k in range(PAIRS)]
-    for k in range(PAIRS):
-        after = pairs[k + 1] if k + 1 < PAIRS else edge
-        before = pairs[k - 1] if k > 0 else edge
-        store(k, jnp.where(low, after, before), pairs[k])
-
-
 def window_builder(out_ref, center, edge, halo_low, halo_high, edge_low, edge_high):
-    planes = center.shape[0]
-
-    def flat(values):
-        return values.reshape(planes * EDGE, values.shape[-1])
-
     def shifted(values, low_row, high_row, tap):
         if tap == 0:
-            return jnp.concatenate([low_row, values[:, : EDGE - 1]], axis=1)
+            return jnp.concatenate([low_row, values[:, :, : EDGE - 1]], axis=2)
         if tap == 2:
-            return jnp.concatenate([values[:, 1:], high_row], axis=1)
+            return jnp.concatenate([values[:, :, 1:], high_row], axis=2)
         return values
 
     def build(tap):
-        moved = flat(shifted(center, halo_low, halo_high, tap))
-        moved_edge = flat(shifted(edge, edge_low, edge_high, tap))
-
-        def store(k, around, pair):
-            rows = pl.ds(k * planes * EDGE, planes * EDGE)
-            base = tap * 2 * PAIR
-            out_ref[rows, base : base + PAIR] = around.astype(jnp.bfloat16)
-            out_ref[rows, base + PAIR : base + 2 * PAIR] = pair.astype(jnp.bfloat16)
-
-        place_windows(store, moved, moved_edge)
+        moved = shifted(center, halo_low, halo_high, tap)
+        outer = shifted(edge, edge_low, edge_high, tap)
+        low = low_lanes(outer.shape)
+        pairs = [moved[..., PAIR * k : PAIR * (k + 1)] for k in range(PAIRS)]
+        around = []
+        for k in range(PAIRS):
+            after = pairs[k + 1] if k + 1 < PAIRS else outer
+            before = pairs[k - 1] if k > 0 else outer
+            around.append(jnp.where(low, after, before))
+        for half, pieces in enumerate((around, pairs)):
+            rows = jnp.stack(pieces, axis=2).reshape(-1, PAIR).astype(jnp.bfloat16)
+            base = (2 * tap + half) * PAIR
+            out_ref[:, base : base + PAIR] = rows
 
     return build
 
 
 def outer_rows(center, y_ref, width):
-    low, high = [], []
+    sides = []
     for side in range(2):
         below = y_ref[side, 0].astype(jnp.float32)[EDGE - 1 :, None, :width]
         level = y_ref[side, 1].astype(jnp.float32)[:, None, :width]
         above = y_ref[side, 2].astype(jnp.float32)[:1, None, :width]
-        (low if side == 0 else high).extend([below, level, above])
-    planes = EDGE + 2
-    low.append(center[:planes, EDGE - 1 :])
-    high = [center[planes:, :1]] + high
-    return jnp.concatenate(low, axis=0), jnp.concatenate(high, axis=0)
-
-
-def sum_taps(result, planes, store):
-    for k in range(PAIRS):
-        for brick in range(2):
-            base = k * planes * EDGE + brick * (planes // 2) * EDGE
-            total = result[base : base + EDGE * EDGE, :PAIR]
-            for a in range(1, 3):
-                start = base + a * EDGE
-                total = total + result[start : start + EDGE * EDGE, a * PAIR : (a + 1) * PAIR]
-            store(brick, k, total.reshape(EDGE, EDGE, PAIR).astype(jnp.bfloat16))
+        sides.append(jnp.concatenate([below, level, above], axis=0))
+    low = jnp.stack([sides[0], center[:, 0, EDGE - 1 :]], axis=1)
+    high = jnp.stack([center[:, 1, :1], sides[1]], axis=1)
+    return low, high
+
+
+def sum_taps(result, store):
+    step = 2 * PAIRS * EDGE
+    count = EDGE * step
+    total = result[:count, :PAIR]
+    for a in range(1, 3):
+        total = total + result[a * step : a * step + count, a * PAIR : (a + 1) * PAIR]
+    total = total.reshape(EDGE, 2, PAIRS, EDGE, PAIR).astype(jnp.bfloat16)
+    for brick in range(2):
+        for k in range(PAIRS):
+            store(brick, k, total[:, brick, k])
 
 
 def turn(tile):
@@ -119,8 +108,6 @@
 ):
     me = lax.axis_index("space")
     core = lax.axis_index("dp")
-    planes = 2 * (EDGE + 2)
-
     if reduce_here:
         fin = tiles_ref
     else:
@@ -230,47 +217,58 @@
     cys[1] = cz[0].astype(jnp.float32)[:, 0].astype(jnp.bfloat16)
     start_halo(c_copies)
 
-    cot_rows = []
-    zero_plane = jnp.zeros((EDGE, PAIR), jnp.float32)
+    loads[3].wait()
+    blank = jnp.zeros((CH, CH), jnp.bfloat16)
+    for a in range(3):
+        for b in range(3):
+            taps = [w_ref[a, b, d] for d in range(3)]
+            for w, slot in enumerate((1, 2, 3, 0)):
+                left = taps[w] if w < 3 else blank
+                right = taps[w - 1] if w > 0 else blank
+                block = jnp.concatenate([left, right], axis=1)
+                row = (b * 4 + slot) * CH
+                wf[row : row + CH, a * PAIR : (a + 1) * PAIR] = block
+                cell, half = ((1, 0), (0, 1), (1, 1), (0, 0))[w]
+                row = (2 - a) * PAIR + cell * CH
+                lane = (2 - b) * 4 * CH + half * PAIR
+                wg[row : row + CH, lane : lane + PAIR] = block
+
+    pieces = []
     for k in range(PAIRS):
-        per_tap = []
-        blocks = [
-            c_ref[0, brick, :, :, k * PAIR : (k + 1) * PAIR].astype(jnp.float32).reshape(EDGE * EDGE, PAIR)
-            for brick in range(2)
-        ]
-        for a in range(3):
-            pieces = []
-            for brick in range(2):
-                pieces += [zero_plane] * a + [blocks[brick]] + [zero_plane] * (2 - a)
-            per_tap.append(jnp.concatenate(pieces, axis=0))
-        cot_rows.append(jnp.concatenate(per_tap, axis=1))
-    ct[...] = jnp.concatenate(cot_rows, axis=0).T.astype(jnp.bfloat16)
+        lanes = slice(k * PAIR, (k + 1) * PAIR)
+        pieces.append(
+            jnp.stack([c_ref[0, b, :, :, lanes].astype(jnp.float32) for b in range(2)], axis=1)
+        )
+    turned = jnp.stack(pieces, axis=2).reshape(-1, PAIR).T
+    step = 2 * PAIRS * EDGE
+    for a in range(3):
+        padded = [jnp.zeros((PAIR, a * step), jnp.float32)] if a > 0 else []
+        padded.append(turned)
+        if a < 2:
+            padded.append(jnp.zeros((PAIR, (2 - a) * step), jnp.float32))
+        ct[a * PAIR : (a + 1) * PAIR] = jnp.concatenate(padded, axis=1).astype(jnp.bfloat16)
 
     wait_halo(f_copies)
 
     def stack(values, x_ref, width):
-        parts = []
-        for brick in range(2):
-            parts.append(x_ref[0, brick].astype(jnp.float32)[None, :, :width])
-            parts.append(values[brick])
-            parts.append(x_ref[1, brick].astype(jnp.float32)[None, :, :width])
-        return jnp.concatenate(parts, axis=0)
+        first = x_ref[0].astype(jnp.float32)[None, ..., :width]
+        last = x_ref[1].astype(jnp.float32)[None, ..., :width]
+        return jnp.concatenate([first, jnp.stack(values, axis=1), last], axis=0)
 
     center = stack([f_ref[0, b].astype(jnp.float32) for b in range(2)], fx, ROWS)
     row_low, row_high = outer_rows(center, fy, ROWS)
 
     def third_edge(values):
         pieces = []
-        half = planes // 2
         for brick in range(2):
-            other = values[(1 - brick) * half : (2 - brick) * half]
+            other = values[:, 1 - brick]
             before = jnp.where(nb_ref[0, brick, 4] >= 0, 1.0, 0.0)
             after = jnp.where(nb_ref[0, brick, 5] >= 0, 1.0, 0.0)
-            low = low_lanes((half, values.shape[1], PAIR))
+            low = low_lanes(other.shape[:-1] + (PAIR,))
             pieces.append(
                 jnp.where(low, other[..., :PAIR] * after, other[..., ROWS - PAIR :] * before)
             )
-        return jnp.concatenate(pieces, axis=0)
+        return jnp.stack(pieces, axis=1)
 
     build_features = window_builder(
         xw, center, third_edge(center), row_low, row_high, third_edge(row_low), third_edge(row_high)
@@ -323,28 +321,6 @@
             if b > 0:
                 scatter(b - 1)
 
-    loads[3].wait()
-    order = (3, 0, 1, 2)
-    blank = jnp.zeros((CH, CH), jnp.bfloat16)
-    for a in range(3):
-        for b in range(3):
-            taps = [w_ref[a, b, d] for d in range(3)]
-            for slot, w in enumerate(order):
-                left = taps[w] if w < 3 else blank
-                right = taps[w - 1] if w > 0 else blank
-                row = b * 4 * CH + slot * CH
-                wf[row : row + CH, a * PAIR : (a + 1) * PAIR] = jnp.concatenate([left, right], axis=1)
-            flip_a, flip_b = 2 - a, 2 - b
-            for cell in range(2):
-                row = flip_a * PAIR + cell * CH
-                for half in range(2):
-                    pieces = []
-                    for w in order[2 * half : 2 * half + 2]:
-                        d = w - cell
-                        pieces.append(taps[2 - d] if 0 <= d <= 2 else blank)
-                    lane = flip_b * 4 * CH + half * PAIR
-                    wg[row : row + CH, lane : lane + PAIR] = jnp.concatenate(pieces, axis=1)
-
     if reduce_here:
         scatter(2)
 
@@ -357,7 +333,7 @@
     def put_response(brick, k, value):
         resp_ref[0, brick, :, :, k * PAIR : (k + 1) * PAIR] = value
 
-    sum_taps(result, planes, put_response)
+    sum_taps(result, put_response)
 
     wait_halo(c_copies)
     wide = stack([cz[b].astype(jnp.float32) for b in range(2)], cx, WIDE)
@@ -411,7 +387,7 @@
     def put_gradient(brick, k, value):
         fg_ref[0, brick, :, :, k * PAIR : (k + 1) * PAIR] = value
 
-    sum_taps(result, planes, put_gradient)
+    sum_taps(result, put_gradient)
 
     if reduce_here:
         for tile in range(OWNED):

time: 25.1 us -> 25.1 us (level)
  no operation moved by 1% of the time
where the time goes in v5:
time: 25.1 us; the launch traced here: 24.9 us
  Pallas kernels  24.3 us (97%)
  between operations  0.64 us (3%)
    pallas_call x1, Pallas kernels, body(): pl.pallas_call(functools.partial(kernel_body, count, reduce_here), out_sh...  23.2 us
    pallas_call x1, Pallas kernels, body(): pl.pallas_call(functools.partial(finish_body, scale), out_shape=(jax.Shap...  1.06 us

profile of v5, /device:TPU:0, one launch (start us, length us, event | category | flops | bytes accessed | tf_op | source)
XLA Modules:
  0.0 24.9 jit_solution(6585314217371184331)
XLA Ops:
  0.6 23.2 %shard_map.67 = (bf16[1,2,8,8,512]{4,3,2,1,0:T(8,128)(2,1)S(1)}, bf16[1,2,8,8,512]{4,3,2,1,0:T(8,128)(2,1)S(1)}, bf16[14,64,128]{2,1,0:T(8,128)(2,1)S(1)}) custom-call(s32[1,2,6]{2,1,0:T(2,128)} %nb_hbm.1, bf16[1,2,8,8,512]{4,3,2,1,0:T(8,128)(2,1)} %f_hbm.1, bf16[1,2,8,8,512]{4,3,2,1,0:T(8,128)(2,1)} %c_hbm.1, bf16[3,3,3,64,64]{4,3,2,1,0:T(8,128)(2,1)} %w_hbm.1), custom_call_target="tpu_custom_call" | custom-call | flops 1000000000 | bytes 2000000 | tf_op jit(solution)/shard_map/pallas_call | solution.py:466
  23.9 1.1 %shard_map.68 = (bf16[1,2,8,8,512]{4,3,2,1,0:T(8,128)(2,1)}, bf16[1,2,8,8,512]{4,3,2,1,0:T(8,128)(2,1)}, f32[3,3,3,64,64]{4,3,2,1,0:T(8,128)}) custom-call(bf16[1,2,8,8,512]{4,3,2,1,0:T(8,128)(2,1)S(1)} %get-tuple-element.6.resp_ref, bf16[1,2,8,8,512]{4,3,2,1,0:T(8,128)(2,1)S(1)} %get-tuple-element.7.fg_ref, bf16[14,64,128]{2,1,0:T(8,128)(2,1)S(1)} %get-tuple-element.8.tiles_ref), custom_call_target="tpu_custom_call" | custom-call | flops 1000000 | bytes 1000000 | tf_op jit(solution)/shard_map/pallas_call | solution.py:509

commit v6 on v5

--- a/solution.py
+++ b/solution.py
@@ -15,16 +15,18 @@
 PAIRS = EDGE // 2
 ROWS = EDGE * CH
 WIDE = ROWS + PAIR
-TILES = 14
-OWNED = TILES // 2
+SLOTS = 8
+OWNERS = 4
+FIRST_OWNER = 2
 MESH = pl.DeviceIdType.MESH
 BATCHES = ((0, 2), (2, 4), (4, 7))
+OWNERS_READY = ((0,), (1,), (2, 3))
 READY = (
     [("late", 0), ("late", 1), ("late", 2), ("early", 0)]
     + [("late", 3), ("late", 4), ("late", 5), ("early", 1)]
     + [("early", 2), ("late", 6), ("late", 7), ("late", 8), ("early", 3), ("early", 4)]
 )
-SPOT = {name: number % 2 * OWNED + number // 2 for number, name in enumerate(READY)}
+SPOT = {name: number % 2 * SLOTS + number // 2 for number, name in enumerate(READY)}
 DIAGONALS = [(side, dx) for side in range(2) for dx in range(3)]
 
 
@@ -215,7 +217,6 @@
         cz[brick, :, :, ROWS:] = edge.astype(jnp.bfloat16)
     cys[0] = cz[1].astype(jnp.float32)[:, EDGE - 1].astype(jnp.bfloat16)
     cys[1] = cz[0].astype(jnp.float32)[:, 0].astype(jnp.bfloat16)
-    start_halo(c_copies)
 
     loads[3].wait()
     blank = jnp.zeros((CH, CH), jnp.bfloat16)
@@ -277,7 +278,7 @@
     low = low_lanes((CH, PAIR))
     core_copies = [
         pltpu.make_async_remote_copy(
-            src_ref=part.at[pl.ds((1 - core) * OWNED + first, last - first)],
+            src_ref=part.at[pl.ds((1 - core) * SLOTS + first, last - first)],
             dst_ref=core_in.at[pl.ds(first, last - first)],
             send_sem=core_send.at[batch], recv_sem=core_recv.at[batch],
             device_id={"dp": 1 - core}, device_id_type=MESH,
@@ -285,19 +286,26 @@
         for batch, (first, last) in enumerate(BATCHES)
     ] if reduce_here else []
 
-    def scatter_copy(tile):
+    def scatter_copy(owner):
         return pltpu.make_async_remote_copy(
-            src_ref=sbuf.at[tile], dst_ref=rbuf.at[me],
-            send_sem=rs_send.at[tile], recv_sem=rs_recv.at[me],
-            device_id={"space": tile}, device_id_type=MESH,
+            src_ref=sbuf.at[pl.ds(2 * owner, 2)], dst_ref=rbuf.at[me],
+            send_sem=rs_send.at[owner], recv_sem=rs_recv.at[me],
+            device_id={"space": FIRST_OWNER + owner}, device_id_type=MESH,
         )
 
     def scatter(batch):
         core_copies[batch].wait_recv()
         for tile in range(*BATCHES[batch]):
-            total = part[core * OWNED + tile] + core_in[tile]
+            total = part[core * SLOTS + tile] + core_in[tile]
             sbuf[tile] = total.astype(jnp.bfloat16)
-            pl.when(me != tile)(scatter_copy(tile).start)
+        for owner in OWNERS_READY[batch]:
+            pl.when(me != FIRST_OWNER + owner)(scatter_copy(owner).start)
+
+    if reduce_here:
+        sbuf[SLOTS - 1] = jnp.zeros((CH, PAIR), jnp.bfloat16)
+    else:
+        for side in range(2):
+            part[side * SLOTS + SLOTS - 1] = jnp.zeros((CH, PAIR), jnp.float32)
 
     first_taps = []
     for b in range(3):
@@ -323,10 +331,7 @@
 
     if reduce_here:
         scatter(2)
-
-        @pl.when(me < OWNED)
-        def _():
-            rbuf[me] = sbuf[me]
+    start_halo(c_copies)
 
     result = jnp.dot(xw[...], wf[...], preferred_element_type=jnp.float32)
 
@@ -334,6 +339,42 @@
         resp_ref[0, brick, :, :, k * PAIR : (k + 1) * PAIR] = value
 
     sum_taps(result, put_response)
+
+    if reduce_here:
+        mine = me - FIRST_OWNER
+        is_owner = (mine >= 0) & (mine < OWNERS)
+
+        def gather_copy(step):
+            spot = fin.at[pl.ds(core * SLOTS + 2 * mine, 2)]
+            return pltpu.make_async_remote_copy(
+                src_ref=spot, dst_ref=spot,
+                send_sem=ag_send.at[step], recv_sem=ag_recv.at[mine],
+                device_id={"space": (me + step) % count}, device_id_type=MESH,
+            )
+
+        def forward_copy(owner, from_core):
+            spot = fin.at[pl.ds(from_core * SLOTS + 2 * owner, 2)]
+            return pltpu.make_async_remote_copy(
+                src_ref=spot, dst_ref=spot,
+                send_sem=fw_send.at[owner], recv_sem=fw_recv.at[owner],
+                device_id={"dp": 1 - core}, device_id_type=MESH,
+            )
+
+        @pl.when(is_owner)
+        def _():
+            total = sbuf[pl.ds(2 * mine, 2)].astype(jnp.float32)
+            for step in range(1, count):
+                source = (me + step) % count
+                pltpu.make_async_remote_copy(
+                    src_ref=sbuf.at[pl.ds(0, 2)], dst_ref=rbuf.at[source],
+                    send_sem=rs_send.at[0], recv_sem=rs_recv.at[source],
+                    device_id={"space": source}, device_id_type=MESH,
+                ).wait_recv()
+                total = total + rbuf[source].astype(jnp.float32)
+            for half in range(2):
+                fin[core * SLOTS + 2 * mine + half] = turn(total[half]).astype(jnp.bfloat16)
+            for step in range(1, count):
+                gather_copy(step).start()
 
     wait_halo(c_copies)
     wide = stack([cz[b].astype(jnp.float32) for b in range(2)], cx, WIDE)
@@ -345,41 +386,6 @@
     for tap in range(3):
         build_cotangent(tap)
 
-    if reduce_here:
-        def gather_copy(step):
-            target = (me + step) % count
-            return pltpu.make_async_remote_copy(
-                src_ref=fin.at[core * OWNED + me], dst_ref=fin.at[core * OWNED + me],
-                send_sem=ag_send.at[step], recv_sem=ag_recv.at[me],
-                device_id={"space": target}, device_id_type=MESH,
-            )
-
-        def forward_copy(tile):
-            spot = fin.at[core * OWNED + tile]
-            return pltpu.make_async_remote_copy(
-                src_ref=spot, dst_ref=spot,
-                send_sem=fw_send.at[tile], recv_sem=fw_recv.at[tile],
-                device_id={"dp": 1 - core}, device_id_type=MESH,
-            )
-
-        @pl.when(me < OWNED)
-        def _():
-            total = jnp.zeros((CH, PAIR), jnp.float32)
-            for source in range(count):
-
-                @pl.when(me != source)
-                def _():
-                    pltpu.make_async_remote_copy(
-                        src_ref=sbuf.at[0], dst_ref=rbuf.at[source],
-                        send_sem=rs_send.at[0], recv_sem=rs_recv.at[source],
-                        device_id={"space": source}, device_id_type=MESH,
-                    ).wait_recv()
-
-                total = total + rbuf[source].astype(jnp.float32)
-            fin[core * OWNED + me] = turn(total).astype(jnp.bfloat16)
-            for step in range(1, count):
-                gather_copy(step).start()
-
     result = lax.dot_general(
         cw[...], wg[...], (((1,), (1,)), ((), ())), preferred_element_type=jnp.float32
     )
@@ -390,41 +396,33 @@
     sum_taps(result, put_gradient)
 
     if reduce_here:
-        for tile in range(OWNED):
-
-            @pl.when(me != tile)
+        for owner in range(OWNERS):
+
+            @pl.when(me != FIRST_OWNER + owner)
             def _():
-                spot = fin.at[core * OWNED + tile]
+                spot = fin.at[pl.ds(core * SLOTS + 2 * owner, 2)]
                 pltpu.make_async_remote_copy(
                     src_ref=spot, dst_ref=spot,
-                    send_sem=ag_send.at[0], recv_sem=ag_recv.at[tile],
-                    device_id={"space": tile}, device_id_type=MESH,
+                    send_sem=ag_send.at[0], recv_sem=ag_recv.at[owner],
+                    device_id={"space": FIRST_OWNER + owner}, device_id_type=MESH,
                 ).wait_recv()
 
-            forward_copy(tile).start()
-
-        for tile in range(OWNED):
-            spot = fin.at[(1 - core) * OWNED + tile]
-            pltpu.make_async_remote_copy(
-                src_ref=spot, dst_ref=spot,
-                send_sem=fw_send.at[tile], recv_sem=fw_recv.at[tile],
-                device_id={"dp": 1 - core}, device_id_type=MESH,
-            ).wait_recv()
-        for tile in range(OWNED):
-            forward_copy(tile).wait_send()
-
-        @pl.when(me < OWNED)
+            forward_copy(owner, core).start()
+        for owner in range(OWNERS):
+            forward_copy(owner, 1 - core).wait_recv()
+        for owner in range(OWNERS):
+            forward_copy(owner, core).wait_send()
+            pl.when(me != FIRST_OWNER + owner)(scatter_copy(owner).wait_send)
+        for copy in core_copies:
+            copy.wait_send()
+
+        @pl.when(is_owner)
         def _():
             for step in range(1, count):
                 gather_copy(step).wait_send()
     else:
-        for tile in range(TILES):
-            part[tile] = turn(part[tile])
-    if reduce_here:
-        for copy in core_copies:
-            copy.wait_send()
-        for tile in range(OWNED):
-            pl.when(me != tile)(scatter_copy(tile).wait_send)
+        for name in READY:
+            part[SPOT[name]] = turn(part[SPOT[name]])
     for sent, _, copy in f_copies + c_copies:
         pl.when(sent)(copy.wait_send)
 
@@ -462,7 +460,7 @@
     dma = pltpu.SemaphoreType.DMA
     vmem = pl.BlockSpec(memory_space=pltpu.VMEM)
     hbm = pl.BlockSpec(memory_space=pltpu.HBM)
-    part_shape = (TILES, CH, PAIR)
+    part_shape = (2 * SLOTS, CH, PAIR)
     response, feature_grad, tiles = pl.pallas_call(
         functools.partial(kernel_body, count, reduce_here),
         out_shape=(
@@ -490,9 +488,9 @@
             pltpu.VMEM((12 * CH, 6 * CH), bf16),
             pltpu.VMEM((6 * CH, 12 * CH), bf16),
             pltpu.VMEM(part_shape, f32),
-            pltpu.VMEM((OWNED, CH, PAIR), f32),
-            pltpu.VMEM((8, CH, PAIR), bf16),
-            pltpu.VMEM((8, CH, PAIR), bf16),
+            pltpu.VMEM((SLOTS, CH, PAIR), f32),
+            pltpu.VMEM((SLOTS, CH, PAIR), bf16),
+            pltpu.VMEM((8, 2, CH, PAIR), bf16),
             dma((4,)), dma((16,)), dma((16,)), dma((3,)), dma((3,)), dma((8,)), dma((8,)),
             dma((8,)), dma((8,)), dma((8,)), dma((8,)),
         ],

time: 25.1 us -> 25.8 us (1.028)
  Pallas kernels: 24.3 us -> 25 us
    pallas_call x1, Pallas kernels: 23.2 us -> 23.9 us  [body(): pl.pallas_call(functools.partial(kernel_body, count, reduce_here), out_sh...]
where the time goes in v6:
time: 25.8 us; the launch traced here: 25.6 us
  Pallas kernels  25 us (97%)
  between operations  0.64 us (2%)
    pallas_call x1, Pallas kernels, body(): pl.pallas_call(functools.partial(kernel_body, count, reduce_here), out_sh...  23.9 us
    pallas_call x1, Pallas kernels, body(): pl.pallas_call(functools.partial(finish_body, scale), out_shape=(jax.Shap...  1.06 us

profile of v6, /device:TPU:0, one launch (start us, length us, event | category | flops | bytes accessed | tf_op | source)
XLA Modules:
  0.0 25.6 jit_solution(4585030236839377747)
XLA Ops:
  0.6 23.9 %shard_map.67 = (bf16[1,2,8,8,512]{4,3,2,1,0:T(8,128)(2,1)S(1)}, bf16[1,2,8,8,512]{4,3,2,1,0:T(8,128)(2,1)S(1)}, bf16[16,64,128]{2,1,0:T(8,128)(2,1)S(1)}) custom-call(s32[1,2,6]{2,1,0:T(2,128)} %nb_hbm.1, bf16[1,2,8,8,512]{4,3,2,1,0:T(8,128)(2,1)} %f_hbm.1, bf16[1,2,8,8,512]{4,3,2,1,0:T(8,128)(2,1)} %c_hbm.1, bf16[3,3,3,64,64]{4,3,2,1,0:T(8,128)(2,1)} %w_hbm.1), custom_call_target="tpu_custom_call" | custom-call | flops 1000000000 | bytes 2000000 | tf_op jit(solution)/shard_map/pallas_call | solution.py:464
  24.6 1.1 %shard_map.68 = (bf16[1,2,8,8,512]{4,3,2,1,0:T(8,128)(2,1)}, bf16[1,2,8,8,512]{4,3,2,1,0:T(8,128)(2,1)}, f32[3,3,3,64,64]{4,3,2,1,0:T(8,128)}) custom-call(bf16[1,2,8,8,512]{4,3,2,1,0:T(8,128)(2,1)S(1)} %get-tuple-element.6.resp_ref, bf16[1,2,8,8,512]{4,3,2,1,0:T(8,128)(2,1)S(1)} %get-tuple-element.7.fg_ref, bf16[16,64,128]{2,1,0:T(8,128)(2,1)S(1)} %get-tuple-element.8.tiles_ref), custom_call_target="tpu_custom_call" | custom-call | flops 1000000 | bytes 1000000 | tf_op jit(solution)/shard_map/pallas_call | solution.py:507

commit v7 on v5

--- a/solution.py
+++ b/solution.py
@@ -215,7 +215,6 @@
         cz[brick, :, :, ROWS:] = edge.astype(jnp.bfloat16)
     cys[0] = cz[1].astype(jnp.float32)[:, EDGE - 1].astype(jnp.bfloat16)
     cys[1] = cz[0].astype(jnp.float32)[:, 0].astype(jnp.bfloat16)
-    start_halo(c_copies)
 
     loads[3].wait()
     blank = jnp.zeros((CH, CH), jnp.bfloat16)
@@ -249,6 +248,7 @@
         ct[a * PAIR : (a + 1) * PAIR] = jnp.concatenate(padded, axis=1).astype(jnp.bfloat16)
 
     wait_halo(f_copies)
+    start_halo(c_copies)
 
     def stack(values, x_ref, width):
         first = x_ref[0].astype(jnp.float32)[None, ..., :width]
@@ -285,19 +285,19 @@
         for batch, (first, last) in enumerate(BATCHES)
     ] if reduce_here else []
 
-    def scatter_copy(tile):
-        return pltpu.make_async_remote_copy(
-            src_ref=sbuf.at[tile], dst_ref=rbuf.at[me],
-            send_sem=rs_send.at[tile], recv_sem=rs_recv.at[me],
-            device_id={"space": tile}, device_id_type=MESH,
+    def scatter_copy(step):
+        target = (me + step) % count
+        return target, pltpu.make_async_remote_copy(
+            src_ref=sbuf.at[target], dst_ref=rbuf.at[me],
+            send_sem=rs_send.at[step], recv_sem=rs_recv.at[me],
+            device_id={"space": target}, device_id_type=MESH,
         )
 
-    def scatter(batch):
+    def add_core(batch):
         core_copies[batch].wait_recv()
         for tile in range(*BATCHES[batch]):
             total = part[core * OWNED + tile] + core_in[tile]
             sbuf[tile] = total.astype(jnp.bfloat16)
-            pl.when(me != tile)(scatter_copy(tile).start)
 
     first_taps = []
     for b in range(3):
@@ -319,14 +319,13 @@
         if reduce_here:
             core_copies[b].start()
             if b > 0:
-                scatter(b - 1)
-
-    if reduce_here:
-        scatter(2)
-
-        @pl.when(me < OWNED)
-        def _():
-            rbuf[me] = sbuf[me]
+                add_core(b - 1)
+
+    if reduce_here:
+        add_core(2)
+        for step in range(1, count):
+            target, copy = scatter_copy(step)
+            pl.when(target < OWNED)(copy.start)
 
     result = jnp.dot(xw[...], wf[...], preferred_element_type=jnp.float32)
 
@@ -364,17 +363,14 @@
 
         @pl.when(me < OWNED)
         def _():
-            total = jnp.zeros((CH, PAIR), jnp.float32)
-            for source in range(count):
-
-                @pl.when(me != source)
-                def _():
-                    pltpu.make_async_remote_copy(
-                        src_ref=sbuf.at[0], dst_ref=rbuf.at[source],
-                        send_sem=rs_send.at[0], recv_sem=rs_recv.at[source],
-                        device_id={"space": source}, device_id_type=MESH,
-                    ).wait_recv()
-
+            total = sbuf[me].astype(jnp.float32)
+            for step in range(1, count):
+                source = (me + step) % count
+                pltpu.make_async_remote_copy(
+                    src_ref=sbuf.at[0], dst_ref=rbuf.at[source],
+                    send_sem=rs_send.at[0], recv_sem=rs_recv.at[source],
+                    device_id={"space": source}, device_id_type=MESH,
+                ).wait_recv()
                 total = total + rbuf[source].astype(jnp.float32)
             fin[core * OWNED + me] = turn(total).astype(jnp.bfloat16)
             for step in range(1, count):
@@ -423,8 +419,9 @@
     if reduce_here:
         for copy in core_copies:
             copy.wait_send()
-        for tile in range(OWNED):
-            pl.when(me != tile)(scatter_copy(tile).wait_send)
+        for step in range(1, count):
+            target, copy = scatter_copy(step)
+            pl.when(target < OWNED)(copy.wait_send)
     for sent, _, copy in f_copies + c_copies:
         pl.when(sent)(copy.wait_send)
 

time: 25.1 us -> 24.8 us (0.988)
  Pallas kernels: 24.3 us -> 24 us
    pallas_call x1, Pallas kernels: 23.2 us -> 22.9 us  [body(): pl.pallas_call(functools.partial(kernel_body, count, reduce_here), out_sh...]
where the time goes in v7:
time: 24.8 us; the launch traced here: 24.6 us
  Pallas kernels  24 us (97%)
  between operations  0.64 us (3%)
    pallas_call x1, Pallas kernels, body(): pl.pallas_call(functools.partial(kernel_body, count, reduce_here), out_sh...  22.9 us
    pallas_call x1, Pallas kernels, body(): pl.pallas_call(functools.partial(finish_body, scale), out_shape=(jax.Shap...  1.06 us

profile of v7, /device:TPU:0, one launch (start us, length us, event | category | flops | bytes accessed | tf_op | source)
XLA Modules:
  0.0 24.6 jit_solution(10298346290417181386)
XLA Ops:
  0.6 22.9 %shard_map.67 = (bf16[1,2,8,8,512]{4,3,2,1,0:T(8,128)(2,1)S(1)}, bf16[1,2,8,8,512]{4,3,2,1,0:T(8,128)(2,1)S(1)}, bf16[14,64,128]{2,1,0:T(8,128)(2,1)S(1)}) custom-call(s32[1,2,6]{2,1,0:T(2,128)} %nb_hbm.1, bf16[1,2,8,8,512]{4,3,2,1,0:T(8,128)(2,1)} %f_hbm.1, bf16[1,2,8,8,512]{4,3,2,1,0:T(8,128)(2,1)} %c_hbm.1, bf16[3,3,3,64,64]{4,3,2,1,0:T(8,128)(2,1)} %w_hbm.1), custom_call_target="tpu_custom_call" | custom-call | flops 1000000000 | bytes 2000000 | tf_op jit(solution)/shard_map/pallas_call | solution.py:463
  23.6 1.1 %shard_map.68 = (bf16[1,2,8,8,512]{4,3,2,1,0:T(8,128)(2,1)}, bf16[1,2,8,8,512]{4,3,2,1,0:T(8,128)(2,1)}, f32[3,3,3,64,64]{4,3,2,1,0:T(8,128)}) custom-call(bf16[1,2,8,8,512]{4,3,2,1,0:T(8,128)(2,1)S(1)} %get-tuple-element.6.resp_ref, bf16[1,2,8,8,512]{4,3,2,1,0:T(8,128)(2,1)S(1)} %get-tuple-element.7.fg_ref, bf16[14,64,128]{2,1,0:T(8,128)(2,1)S(1)} %get-tuple-element.8.tiles_ref), custom_call_target="tpu_custom_call" | custom-call | flops 1000000 | bytes 1000000 | tf_op jit(solution)/shard_map/pallas_call | solution.py:506

commit v8 on v7

--- a/solution.py
+++ b/solution.py
@@ -344,6 +344,15 @@
     for tap in range(3):
         build_cotangent(tap)
 
+    result = lax.dot_general(
+        cw[...], wg[...], (((1,), (1,)), ((), ())), preferred_element_type=jnp.float32
+    )
+
+    def put_gradient(brick, k, value):
+        fg_ref[0, brick, :, :, k * PAIR : (k + 1) * PAIR] = value
+
+    sum_taps(result, put_gradient)
+
     if reduce_here:
         def gather_copy(step):
             target = (me + step) % count
@@ -376,14 +385,6 @@
             for step in range(1, count):
                 gather_copy(step).start()
 
-    result = lax.dot_general(
-        cw[...], wg[...], (((1,), (1,)), ((), ())), preferred_element_type=jnp.float32
-    )
-
-    def put_gradient(brick, k, value):
-        fg_ref[0, brick, :, :, k * PAIR : (k + 1) * PAIR] = value
-
-    sum_taps(result, put_gradient)
 
     if reduce_here:
         for tile in range(OWNED):

time: 24.8 us -> 24.8 us (level)
  no operation moved by 1% of the time
where the time goes in v8:
time: 24.8 us; the launch traced here: 24.6 us
  Pallas kernels  24 us (97%)
  between operations  0.64 us (3%)
    pallas_call x1, Pallas kernels, body(): pl.pallas_call(functools.partial(kernel_body, count, reduce_here), out_sh...  22.9 us
    pallas_call x1, Pallas kernels, body(): pl.pallas_call(functools.partial(finish_body, scale), out_shape=(jax.Shap...  1.06 us

profile of v8, /device:TPU:0, one launch (start us, length us, event | category | flops | bytes accessed | tf_op | source)
XLA Modules:
  0.0 24.6 jit_solution(17671830380116405495)
XLA Ops:
  0.6 22.9 %shard_map.67 = (bf16[1,2,8,8,512]{4,3,2,1,0:T(8,128)(2,1)S(1)}, bf16[1,2,8,8,512]{4,3,2,1,0:T(8,128)(2,1)S(1)}, bf16[14,64,128]{2,1,0:T(8,128)(2,1)S(1)}) custom-call(s32[1,2,6]{2,1,0:T(2,128)} %nb_hbm.1, bf16[1,2,8,8,512]{4,3,2,1,0:T(8,128)(2,1)} %f_hbm.1, bf16[1,2,8,8,512]{4,3,2,1,0:T(8,128)(2,1)} %c_hbm.1, bf16[3,3,3,64,64]{4,3,2,1,0:T(8,128)(2,1)} %w_hbm.1), custom_call_target="tpu_custom_call" | custom-call | flops 1000000000 | bytes 2000000 | tf_op jit(solution)/shard_map/pallas_call | solution.py:464
  23.6 1.1 %shard_map.68 = (bf16[1,2,8,8,512]{4,3,2,1,0:T(8,128)(2,1)}, bf16[1,2,8,8,512]{4,3,2,1,0:T(8,128)(2,1)}, f32[3,3,3,64,64]{4,3,2,1,0:T(8,128)}) custom-call(bf16[1,2,8,8,512]{4,3,2,1,0:T(8,128)(2,1)S(1)} %get-tuple-element.6.resp_ref, bf16[1,2,8,8,512]{4,3,2,1,0:T(8,128)(2,1)S(1)} %get-tuple-element.7.fg_ref, bf16[14,64,128]{2,1,0:T(8,128)(2,1)S(1)} %get-tuple-element.8.tiles_ref), custom_call_target="tpu_custom_call" | custom-call | flops 1000000 | bytes 1000000 | tf_op jit(solution)/shard_map/pallas_call | solution.py:507

commit v9 on v8

--- a/solution.py
+++ b/solution.py
@@ -293,6 +293,11 @@
             device_id={"space": target}, device_id_type=MESH,
         )
 
+    def scatter(first, last):
+        for step in range(1, count):
+            target, copy = scatter_copy(step)
+            pl.when((target >= first) & (target < last))(copy.start)
+
     def add_core(batch):
         core_copies[batch].wait_recv()
         for tile in range(*BATCHES[batch]):
@@ -320,12 +325,12 @@
             core_copies[b].start()
             if b > 0:
                 add_core(b - 1)
+    if reduce_here:
+        scatter(0, BATCHES[1][1])
 
     if reduce_here:
         add_core(2)
-        for step in range(1, count):
-            target, copy = scatter_copy(step)
-            pl.when(target < OWNED)(copy.start)
+        scatter(BATCHES[1][1], OWNED)
 
     result = jnp.dot(xw[...], wf[...], preferred_element_type=jnp.float32)
 

time: 24.8 us -> 24.7 us (level)
  no operation moved by 1% of the time
where the time goes in v9:
time: 24.7 us; the launch traced here: 24.6 us
  Pallas kernels  23.9 us (97%)
  between operations  0.64 us (3%)
    pallas_call x1, Pallas kernels, body(): pl.pallas_call(functools.partial(kernel_body, count, reduce_here), out_sh...  22.9 us
    pallas_call x1, Pallas kernels, body(): pl.pallas_call(functools.partial(finish_body, scale), out_shape=(jax.Shap...  1.06 us

profile of v9, /device:TPU:0, one launch (start us, length us, event | category | flops | bytes accessed | tf_op | source)
XLA Modules:
  0.0 24.6 jit_solution(11402105727131054877)
XLA Ops:
  0.6 22.9 %shard_map.67 = (bf16[1,2,8,8,512]{4,3,2,1,0:T(8,128)(2,1)S(1)}, bf16[1,2,8,8,512]{4,3,2,1,0:T(8,128)(2,1)S(1)}, bf16[14,64,128]{2,1,0:T(8,128)(2,1)S(1)}) custom-call(s32[1,2,6]{2,1,0:T(2,128)} %nb_hbm.1, bf16[1,2,8,8,512]{4,3,2,1,0:T(8,128)(2,1)} %f_hbm.1, bf16[1,2,8,8,512]{4,3,2,1,0:T(8,128)(2,1)} %c_hbm.1, bf16[3,3,3,64,64]{4,3,2,1,0:T(8,128)(2,1)} %w_hbm.1), custom_call_target="tpu_custom_call" | custom-call | flops 1000000000 | bytes 2000000 | tf_op jit(solution)/shard_map/pallas_call | solution.py:469
  23.5 1.1 %shard_map.68 = (bf16[1,2,8,8,512]{4,3,2,1,0:T(8,128)(2,1)}, bf16[1,2,8,8,512]{4,3,2,1,0:T(8,128)(2,1)}, f32[3,3,3,64,64]{4,3,2,1,0:T(8,128)}) custom-call(bf16[1,2,8,8,512]{4,3,2,1,0:T(8,128)(2,1)S(1)} %get-tuple-element.6.resp_ref, bf16[1,2,8,8,512]{4,3,2,1,0:T(8,128)(2,1)S(1)} %get-tuple-element.7.fg_ref, bf16[14,64,128]{2,1,0:T(8,128)(2,1)S(1)} %get-tuple-element.8.tiles_ref), custom_call_target="tpu_custom_call" | custom-call | flops 1000000 | bytes 1000000 | tf_op jit(solution)/shard_map/pallas_call | solution.py:512
